TPU v7x, 128 devices: a whole 4x4x4 slice. The times are simulated.
128 devices in a mesh: section: 2 (over core), ctx: 8 (over y_hi, x), head: 8 (over z, y_lo).
Axes of the slice: x: 4, y: 4 (y_hi: 2, y_lo: 2; y = y_hi * 2 + y_lo), z: 4, core: 2. Of those that a mesh axis runs over, the one named last changes fastest.
Arguments:
- prompt_query: bfloat16 [4, 4096, 8192], P('section', 'ctx', 'head'), may hold values from -8 to 8
- prompt_key: bfloat16 [4, 4096, 1024], P('section', 'ctx', 'head'), may hold values from -8 to 8
- prompt_value: bfloat16 [4, 4096, 1024], P('section', 'ctx', 'head'), may hold values from -6 to 6
- step_query: bfloat16 [512, 8192], P(('section', 'ctx'), 'head'), may hold values from -8 to 8
- cache_key: bfloat16 [512, 1024, 1024], P(('section', 'ctx'), None, 'head'), may hold values from -8 to 8
- cache_value: bfloat16 [512, 1024, 1024], P(('section', 'ctx'), None, 'head'), may hold values from -6 to 6
- cache_length: int32 [512], P(('section', 'ctx')), may hold values from 1 to 1024
- owner_slots: int32 [16, 2], replicated, may hold values from 0 to 3, as said below
- request_slot: int32 [512], P(('section', 'ctx')), may hold values from 0 to 1
Outputs:
- prompt_context: bfloat16 [4, 4096, 8192], P('section', 'ctx', 'head')
- step_context: bfloat16 [512, 8192], P(('section', 'ctx'), 'head')
Inputs may be any that keep to these rules, and one draw needn't show every extreme that they name: `owner_slots`: each row lists 2 different prompts.
All inputs are finite; a program needn't handle non-finite values.
Results may differ from a plain program's by a relative error of at most 0.015.
Values may be sent and summed in bfloat16 or wider, within the bound.
A program may use at most 128 MiB of HBM per device.

v0:
```python
import jax
import jax.numpy as jnp
from jax import lax
from jax.sharding import PartitionSpec as P

HEADS = 64
KV_HEADS = 8
HEAD_DIM = 128


FLOOR = -1e30


def attend_block(queries, query_start, running, key_block, value_block, first_key):
    maxima, totals, summed = running
    kv_local = queries.shape[2]
    key_rows = key_block.shape[1]
    score_scale = queries.shape[-1] ** (-0.5)
    key_block = key_block.reshape(key_block.shape[0], key_rows, kv_local, -1)
    value_block = value_block.reshape(value_block.shape[0], key_rows, kv_local, -1)
    scores = (
        jnp.einsum("pqkgd,pnkd->pkgqn", queries, key_block, preferred_element_type=jnp.float32)
        * score_scale
    )
    query_pos = query_start + lax.broadcasted_iota(jnp.int32, (queries.shape[1], key_rows), 0)
    key_pos = first_key + lax.broadcasted_iota(jnp.int32, (queries.shape[1], key_rows), 1)
    allowed = key_pos <= query_pos
    scores = jnp.where(allowed, scores, FLOOR)
    new_max = jnp.maximum(maxima, jnp.max(scores, axis=-1))
    weights = jnp.where(allowed, jnp.exp(scores - new_max[..., None]), 0.0).astype(jnp.bfloat16)
    factor = jnp.exp(maxima - new_max)
    totals = totals * factor + jnp.sum(weights, axis=-1, dtype=jnp.float32)
    summed = summed * factor[..., None] + jnp.einsum(
        "pkgqn,pnkd->pkgqd", weights, value_block, preferred_element_type=jnp.float32
    )
    return (new_max, totals, summed)


def prompt_attend(queries, query_start, running, pieces):
    key_rows = pieces[0].shape[1]
    block_rows = 512
    last_query = query_start + queries.shape[1] - 1

    def advance(state_now, block_index):
        offset = block_index * block_rows
        key_block = lax.dynamic_slice_in_dim(pieces[0], offset, block_rows, 1)
        value_block = lax.dynamic_slice_in_dim(pieces[1], offset, block_rows, 1)

        def compute(state_in):
            return attend_block(queries, query_start, state_in, key_block, value_block, offset)

        def keep(state_in):
            return state_in

        return (lax.cond(offset <= last_query, compute, keep, state_now), None)

    result, _ = lax.scan(advance, running, jnp.arange(key_rows // block_rows, dtype=jnp.int32))
    return result


def on_device(
    prompt_query,
    prompt_key,
    prompt_value,
    step_query,
    cache_key,
    cache_value,
    cache_length,
    owner_slots,
    request_slot,
):
    local_prompts, shard_len, query_width = prompt_query.shape
    key_width = prompt_key.shape[2]
    kv_local = key_width // HEAD_DIM
    group_size = HEADS // KV_HEADS
    ctx_count = lax.axis_size("ctx")
    section_index = lax.axis_index("section")
    ctx_index = lax.axis_index("ctx")
    slots_count = owner_slots.shape[1]
    queries = prompt_query.reshape(local_prompts, shard_len, kv_local, group_size, HEAD_DIM)
    query_start = ctx_index * shard_len
    row_shape = (local_prompts, kv_local, group_size, shard_len)
    initial = (
        jnp.full(row_shape, FLOOR, jnp.float32),
        jnp.zeros(row_shape, jnp.float32),
        jnp.zeros(row_shape + (HEAD_DIM,), jnp.float32),
    )
    prompt_ids = section_index * local_prompts + jnp.arange(local_prompts, dtype=jnp.int32)
    maxima, totals, summed = prompt_attend(
        queries,
        query_start,
        initial,
        (
            lax.all_gather(prompt_key, "ctx", axis=1, tiled=True),
            lax.all_gather(prompt_value, "ctx", axis=1, tiled=True),
        ),
    )
    context = summed / totals[..., None]
    prompt_context = (
        jnp.transpose(context, (0, 3, 1, 2, 4))
        .reshape(local_prompts, shard_len, query_width)
        .astype(jnp.bfloat16)
    )
    requests = step_query.shape[0]
    score_scale = HEAD_DIM ** (-0.5)
    step_queries = step_query.reshape(requests, kv_local, group_size, HEAD_DIM)
    cached_keys = cache_key.reshape(requests, -1, kv_local, HEAD_DIM)
    cached_values = cache_value.reshape(requests, -1, kv_local, HEAD_DIM)
    cache_scores = (
        jnp.einsum("rkgd,rnkd->rkgn", step_queries, cached_keys, preferred_element_type=jnp.float32)
        * score_scale
    )
    inside = (
        lax.broadcasted_iota(jnp.int32, (requests, cached_keys.shape[1]), 1) < cache_length[:, None]
    )
    inside = inside[:, None, None, :]
    cache_scores = jnp.where(inside, cache_scores, FLOOR)
    local_pairs = jnp.concatenate([prompt_key, prompt_value], axis=2)
    picked = (owner_slots[:, :, None] == prompt_ids[None, None, :]).astype(jnp.bfloat16)
    outgoing = jnp.einsum(
        "oti,isc->otsc", picked, local_pairs, preferred_element_type=jnp.float32
    ).astype(jnp.bfloat16)
    incoming = lax.all_to_all(outgoing, ("section", "ctx"), split_axis=0, concat_axis=0, tiled=True)
    owner_count = incoming.shape[0]
    incoming = incoming.reshape(
        owner_count // ctx_count, ctx_count, slots_count, shard_len, 2 * key_width
    )
    merged = jnp.sum(incoming, axis=0)
    persona = jnp.transpose(merged, (1, 0, 2, 3)).reshape(
        slots_count, ctx_count * shard_len, 2 * key_width
    )
    persona_keys = persona[:, :, :key_width].reshape(slots_count, -1, kv_local, HEAD_DIM)
    persona_values = persona[:, :, key_width:].reshape(slots_count, -1, kv_local, HEAD_DIM)
    persona_scores = (
        jnp.einsum(
            "rkgd,tnkd->rkgtn", step_queries, persona_keys, preferred_element_type=jnp.float32
        )
        * score_scale
    )
    chosen = (request_slot[:, None] == jnp.arange(slots_count, dtype=jnp.int32)[None, :])[
        :, None, None, :, None
    ]
    persona_scores = jnp.where(chosen, persona_scores, FLOOR)
    highest = jnp.maximum(jnp.max(cache_scores, axis=-1), jnp.max(persona_scores, axis=(-2, -1)))
    cache_weights = jnp.where(inside, jnp.exp(cache_scores - highest[..., None]), 0.0).astype(
        jnp.bfloat16
    )
    persona_weights = jnp.where(
        chosen, jnp.exp(persona_scores - highest[..., None, None]), 0.0
    ).astype(jnp.bfloat16)
    denominator = jnp.sum(cache_weights, axis=-1, dtype=jnp.float32) + jnp.sum(
        persona_weights, axis=(-2, -1), dtype=jnp.float32
    )
    weighted = jnp.einsum(
        "rkgn,rnkd->rkgd", cache_weights, cached_values, preferred_element_type=jnp.float32
    )
    weighted = weighted + jnp.einsum(
        "rkgtn,tnkd->rkgd", persona_weights, persona_values, preferred_element_type=jnp.float32
    )
    weighted, denominator = (weighted, denominator)
    step_context = (
        (weighted / denominator[..., None])
        .reshape(requests, kv_local * group_size * HEAD_DIM)
        .astype(jnp.bfloat16)
    )
    return (prompt_context, step_context)


def solution(mesh):
    in_specs = (
        P("section", "ctx", "head"),
        P("section", "ctx", "head"),
        P("section", "ctx", "head"),
        P(("section", "ctx"), "head"),
        P(("section", "ctx"), None, "head"),
        P(("section", "ctx"), None, "head"),
        P(("section", "ctx")),
        P(),
        P(("section", "ctx")),
    )
    out_specs = (P("section", "ctx", "head"), P(("section", "ctx"), "head"))
    return jax.shard_map(
        on_device, mesh=mesh, in_specs=in_specs, out_specs=out_specs, check_vma=False
    )
```

profile of v0, /device:TPU:30, one launch (start us, length us, event | category | flops | bytes accessed | tf_op | source)
XLA Modules:
  0.0 394.0 jit_solution(5810101415337866041)
XLA Ops:
  10.4 5.8 %convolution_convert_fusion = bf16[16,2,512,256]{3,0,2,1:T(8,128)(2,1)} fusion(bf16[2,512,128]{2,0,1:T(2,128)(2,1)S(1)} %copy.63, bf16[2,512,128]{2,0,1:T(2,128)(2,1)S(1)} %copy.62, s32[16,2]{0,1:T(2,128)} %param.20, s32[2]{0:T(128)S(1)} %iota_add_fusion.2), kind=kOutput, calls=%fused_computation.29 | convolution fusion | flops 22020160 | bytes 8913032 | tf_op jit(solution)/shard_map/oti,isc->otsc/dot_general | solution.py:120
  16.2 9.6 %copy.64 = bf16[16,2,512,256]{3,2,1,0:T(8,128)(2,1)} copy(bf16[16,2,512,256]{3,0,2,1:T(8,128)(2,1)} %convolution_convert_fusion) | data formatting | bytes 16777216 | tf_op jit(solution)/shard_map/convert_element_type | solution.py:122
  25.8 7.3 %all-to-all-start = ((bf16[16,2,512,256]{3,2,1,0:T(8,128)(2,1)}), bf16[16,2,512,256]{3,2,1,0:T(8,128)(2,1)}, u32[]{:S(2)}, u32[]{:S(2)}) async-start(bf16[16,2,512,256]{3,2,1,0:T(8,128)(2,1)} %copy.64), calls=%async_computation | async-start | bytes 16777216 | tf_op jit(solution)/shard_map/all_to_all | solution.py:123
  33.9 2.6 copy.59
  36.5 3.0 copy.60
  39.7 6.7 %fusion.39 = (f32[32,8]{1,0:T(8,128)S(1)}, f32[32,8,1024]{2,1,0:T(8,128)}) fusion(bf16[32,8,128]{2,1,0:T(8,128)(2,1)S(1)} %bitcast.140, bf16[32,1024,128]{2,1,0:T(8,128)(2,1)} %param.17, pred[32,1024]{1,0:T(8,128)(4,1)S(1)} %iota_compare_fusion), kind=kOutput, calls=%fused_computation.62 | convolution fusion | flops 67895040 | bytes 9536512 | tf_op jit(solution)/shard_map/rkgd,rnkd->rkgn/dot_general | solution.py:110
  46.5 99.3 %all-gather.3.cloned.1.call-done = bf16[2,4096,128]{2,1,0:T(8,128)(2,1)} async-done(((bf16[2,512,128]{2,1,0:T(8,128)(2,1)}), bf16[2,4096,128]{2,1,0:T(8,128)(2,1)}) %all-gather.3.cloned.1.call-update) | async-done | bytes 2097168 | tf_op jit(solution)/shard_map/all_gather | solution.py:94
  145.7 57.4 %all-gather.5.cloned.1.call-done = bf16[2,4096,128]{2,1,0:T(8,128)(2,1)} async-done(((bf16[2,512,128]{2,1,0:T(8,128)(2,1)}), bf16[2,4096,128]{2,1,0:T(8,128)(2,1)}) %all-gather.5.cloned.1.call-update) | async-done | bytes 2097168 | tf_op jit(solution)/shard_map/all_gather | solution.py:95
  205.5 144.5 %while.14 = (s32[]{:T(128)}, f32[2,1,8,512]{3,2,0,1:T(8,128)S(1)}, f32[2,1,8,512]{3,2,0,1:T(8,128)S(1)}, f32[2,1,8,512,128]{4,3,2,0,1:T(8,128)}, s32[8]{0:T(128)...) while((s32[]{:T(128)}, f32[2,1,8,512]{3,2,0,1:T(8,128)S(1)}, ...), condition=%wide.region_5.6_spmd, body=%wide.region_0.5_spmd.sunk | while | flops 2212783104 | bytes 62923088 | solution.py:57
  206.6 16.9 %conditional.2 = ((f32[2,1,8,512]{3,2,0,1:T(8,128)S(1)}, f32[2,1,8,512]{3,2,0,1:T(8,128)S(1)}, f32[2,1,8,512,128]{4,3,2,0,1:T(8,128)})) conditional(s32[]{:T(128)} %convert_element_type.84, (f32[2,1,8,512]{3,2,0,1:T(8,128)S(1)}, f32[2,1,8,512]{3,2,0,1:T(8,128)S(1)}, f32[2,1,8,512,128]{4,3,2,0,1:T(8,128)}) %tuple.50, (s32[]{:T(128)}, s32[]{:T(128)}, ...), branch_computations={%region_1.1_spmd, %region_2.4_spmd} | conditional | flops 2212783104 | bytes 62922836 | solution.py:55
  206.9 3.9 fusion
  210.8 4.0 %convert_reduce_fusion = f32[2,8,512]{2,1,0:T(8,128)S(1)} fusion(f32[2,8,512]{2,1,0:T(8,128)S(1)} %bitcast.133, f32[2,512,512,8]{2,1,3,0:T(8,128)S(1)} %get-tuple-element.227, pred[512,512]{0,1:T(8,128)(4,1)S(1)} %broadcast_compare_fusion), kind=kLoop, calls=%fused_computation.1 | loop fusion | flops 29351936 | bytes 17104896 | tf_op jit(solution)/shard_map/while/body/eval_jaxpr/cond/branch_1_fun/reduce_sum | solution.py:32
  214.9 8.7 %bitcast_add_fusion = f32[2,1,8,512,128]{4,3,2,0,1:T(8,128)} fusion(f32[2,1,8,512,128]{4,3,2,0,1:T(8,128)} %get-tuple-element.142, f32[2,8,512]{2,1,0:T(8,128)S(1)} %get-tuple-element.224, bf16[2,4096,128]{2,1,0:T(8,128)(2,1)} %get-tuple-element.143, s32[]{:T(128)S(6)} %select_n.28, f32[2,512,512,8]{2,1,3,0:T(8,128)S(1)} %get-tuple-element.227, ...), kind=kOutput, calls=%fused_computation.6 | convolution fusion | flops 1096810496 | bytes 25755652 | tf_op jit(solution)/shard_map/while/body/eval_jaxpr/cond/branch_1_fun/pkgqn,pnkd->pkgqd/dot_general | solution.py:33
  224.7 16.9 %conditional.2 = ((f32[2,1,8,512]{3,2,0,1:T(8,128)S(1)}, f32[2,1,8,512]{3,2,0,1:T(8,128)S(1)}, f32[2,1,8,512,128]{4,3,2,0,1:T(8,128)})) conditional(s32[]{:T(128)} %convert_element_type.84, (f32[2,1,8,512]{3,2,0,1:T(8,128)S(1)}, f32[2,1,8,512]{3,2,0,1:T(8,128)S(1)}, f32[2,1,8,512,128]{4,3,2,0,1:T(8,128)}) %tuple.50, (s32[]{:T(128)}, s32[]{:T(128)}, ...), branch_computations={%region_1.1_spmd, %region_2.4_spmd} | conditional | flops 2212783104 | bytes 62922836 | solution.py:55
  225.0 3.9 fusion
  228.9 4.0 %convert_reduce_fusion = f32[2,8,512]{2,1,0:T(8,128)S(1)} fusion(f32[2,8,512]{2,1,0:T(8,128)S(1)} %bitcast.133, f32[2,512,512,8]{2,1,3,0:T(8,128)S(1)} %get-tuple-element.227, pred[512,512]{0,1:T(8,128)(4,1)S(1)} %broadcast_compare_fusion), kind=kLoop, calls=%fused_computation.1 | loop fusion | flops 29351936 | bytes 17104896 | tf_op jit(solution)/shard_map/while/body/eval_jaxpr/cond/branch_1_fun/reduce_sum | solution.py:32
  232.9 8.7 %bitcast_add_fusion = f32[2,1,8,512,128]{4,3,2,0,1:T(8,128)} fusion(f32[2,1,8,512,128]{4,3,2,0,1:T(8,128)} %get-tuple-element.142, f32[2,8,512]{2,1,0:T(8,128)S(1)} %get-tuple-element.224, bf16[2,4096,128]{2,1,0:T(8,128)(2,1)} %get-tuple-element.143, s32[]{:T(128)S(6)} %select_n.28, f32[2,512,512,8]{2,1,3,0:T(8,128)S(1)} %get-tuple-element.227, ...), kind=kOutput, calls=%fused_computation.6 | convolution fusion | flops 1096810496 | bytes 25755652 | tf_op jit(solution)/shard_map/while/body/eval_jaxpr/cond/branch_1_fun/pkgqn,pnkd->pkgqd/dot_general | solution.py:33
  242.8 16.9 %conditional.2 = ((f32[2,1,8,512]{3,2,0,1:T(8,128)S(1)}, f32[2,1,8,512]{3,2,0,1:T(8,128)S(1)}, f32[2,1,8,512,128]{4,3,2,0,1:T(8,128)})) conditional(s32[]{:T(128)} %convert_element_type.84, (f32[2,1,8,512]{3,2,0,1:T(8,128)S(1)}, f32[2,1,8,512]{3,2,0,1:T(8,128)S(1)}, f32[2,1,8,512,128]{4,3,2,0,1:T(8,128)}) %tuple.50, (s32[]{:T(128)}, s32[]{:T(128)}, ...), branch_computations={%region_1.1_spmd, %region_2.4_spmd} | conditional | flops 2212783104 | bytes 62922836 | solution.py:55
  243.0 3.9 fusion
  246.9 4.0 %convert_reduce_fusion = f32[2,8,512]{2,1,0:T(8,128)S(1)} fusion(f32[2,8,512]{2,1,0:T(8,128)S(1)} %bitcast.133, f32[2,512,512,8]{2,1,3,0:T(8,128)S(1)} %get-tuple-element.227, pred[512,512]{0,1:T(8,128)(4,1)S(1)} %broadcast_compare_fusion), kind=kLoop, calls=%fused_computation.1 | loop fusion | flops 29351936 | bytes 17104896 | tf_op jit(solution)/shard_map/while/body/eval_jaxpr/cond/branch_1_fun/reduce_sum | solution.py:32
  251.0 8.7 %bitcast_add_fusion = f32[2,1,8,512,128]{4,3,2,0,1:T(8,128)} fusion(f32[2,1,8,512,128]{4,3,2,0,1:T(8,128)} %get-tuple-element.142, f32[2,8,512]{2,1,0:T(8,128)S(1)} %get-tuple-element.224, bf16[2,4096,128]{2,1,0:T(8,128)(2,1)} %get-tuple-element.143, s32[]{:T(128)S(6)} %select_n.28, f32[2,512,512,8]{2,1,3,0:T(8,128)S(1)} %get-tuple-element.227, ...), kind=kOutput, calls=%fused_computation.6 | convolution fusion | flops 1096810496 | bytes 25755652 | tf_op jit(solution)/shard_map/while/body/eval_jaxpr/cond/branch_1_fun/pkgqn,pnkd->pkgqd/dot_general | solution.py:33
  260.8 16.9 %conditional.2 = ((f32[2,1,8,512]{3,2,0,1:T(8,128)S(1)}, f32[2,1,8,512]{3,2,0,1:T(8,128)S(1)}, f32[2,1,8,512,128]{4,3,2,0,1:T(8,128)})) conditional(s32[]{:T(128)} %convert_element_type.84, (f32[2,1,8,512]{3,2,0,1:T(8,128)S(1)}, f32[2,1,8,512]{3,2,0,1:T(8,128)S(1)}, f32[2,1,8,512,128]{4,3,2,0,1:T(8,128)}) %tuple.50, (s32[]{:T(128)}, s32[]{:T(128)}, ...), branch_computations={%region_1.1_spmd, %region_2.4_spmd} | conditional | flops 2212783104 | bytes 62922836 | solution.py:55
  261.1 3.9 fusion
  265.0 4.0 %convert_reduce_fusion = f32[2,8,512]{2,1,0:T(8,128)S(1)} fusion(f32[2,8,512]{2,1,0:T(8,128)S(1)} %bitcast.133, f32[2,512,512,8]{2,1,3,0:T(8,128)S(1)} %get-tuple-element.227, pred[512,512]{0,1:T(8,128)(4,1)S(1)} %broadcast_compare_fusion), kind=kLoop, calls=%fused_computation.1 | loop fusion | flops 29351936 | bytes 17104896 | tf_op jit(solution)/shard_map/while/body/eval_jaxpr/cond/branch_1_fun/reduce_sum | solution.py:32
  269.1 8.7 %bitcast_add_fusion = f32[2,1,8,512,128]{4,3,2,0,1:T(8,128)} fusion(f32[2,1,8,512,128]{4,3,2,0,1:T(8,128)} %get-tuple-element.142, f32[2,8,512]{2,1,0:T(8,128)S(1)} %get-tuple-element.224, bf16[2,4096,128]{2,1,0:T(8,128)(2,1)} %get-tuple-element.143, s32[]{:T(128)S(6)} %select_n.28, f32[2,512,512,8]{2,1,3,0:T(8,128)S(1)} %get-tuple-element.227, ...), kind=kOutput, calls=%fused_computation.6 | convolution fusion | flops 1096810496 | bytes 25755652 | tf_op jit(solution)/shard_map/while/body/eval_jaxpr/cond/branch_1_fun/pkgqn,pnkd->pkgqd/dot_general | solution.py:33
  278.9 16.9 %conditional.2 = ((f32[2,1,8,512]{3,2,0,1:T(8,128)S(1)}, f32[2,1,8,512]{3,2,0,1:T(8,128)S(1)}, f32[2,1,8,512,128]{4,3,2,0,1:T(8,128)})) conditional(s32[]{:T(128)} %convert_element_type.84, (f32[2,1,8,512]{3,2,0,1:T(8,128)S(1)}, f32[2,1,8,512]{3,2,0,1:T(8,128)S(1)}, f32[2,1,8,512,128]{4,3,2,0,1:T(8,128)}) %tuple.50, (s32[]{:T(128)}, s32[]{:T(128)}, ...), branch_computations={%region_1.1_spmd, %region_2.4_spmd} | conditional | flops 2212783104 | bytes 62922836 | solution.py:55
  279.1 3.9 fusion
  283.1 4.0 %convert_reduce_fusion = f32[2,8,512]{2,1,0:T(8,128)S(1)} fusion(f32[2,8,512]{2,1,0:T(8,128)S(1)} %bitcast.133, f32[2,512,512,8]{2,1,3,0:T(8,128)S(1)} %get-tuple-element.227, pred[512,512]{0,1:T(8,128)(4,1)S(1)} %broadcast_compare_fusion), kind=kLoop, calls=%fused_computation.1 | loop fusion | flops 29351936 | bytes 17104896 | tf_op jit(solution)/shard_map/while/body/eval_jaxpr/cond/branch_1_fun/reduce_sum | solution.py:32
  287.1 8.7 %bitcast_add_fusion = f32[2,1,8,512,128]{4,3,2,0,1:T(8,128)} fusion(f32[2,1,8,512,128]{4,3,2,0,1:T(8,128)} %get-tuple-element.142, f32[2,8,512]{2,1,0:T(8,128)S(1)} %get-tuple-element.224, bf16[2,4096,128]{2,1,0:T(8,128)(2,1)} %get-tuple-element.143, s32[]{:T(128)S(6)} %select_n.28, f32[2,512,512,8]{2,1,3,0:T(8,128)S(1)} %get-tuple-element.227, ...), kind=kOutput, calls=%fused_computation.6 | convolution fusion | flops 1096810496 | bytes 25755652 | tf_op jit(solution)/shard_map/while/body/eval_jaxpr/cond/branch_1_fun/pkgqn,pnkd->pkgqd/dot_general | solution.py:33
  296.9 16.9 %conditional.2 = ((f32[2,1,8,512]{3,2,0,1:T(8,128)S(1)}, f32[2,1,8,512]{3,2,0,1:T(8,128)S(1)}, f32[2,1,8,512,128]{4,3,2,0,1:T(8,128)})) conditional(s32[]{:T(128)} %convert_element_type.84, (f32[2,1,8,512]{3,2,0,1:T(8,128)S(1)}, f32[2,1,8,512]{3,2,0,1:T(8,128)S(1)}, f32[2,1,8,512,128]{4,3,2,0,1:T(8,128)}) %tuple.50, (s32[]{:T(128)}, s32[]{:T(128)}, ...), branch_computations={%region_1.1_spmd, %region_2.4_spmd} | conditional | flops 2212783104 | bytes 62922836 | solution.py:55
  297.2 3.9 fusion
  301.1 4.0 %convert_reduce_fusion = f32[2,8,512]{2,1,0:T(8,128)S(1)} fusion(f32[2,8,512]{2,1,0:T(8,128)S(1)} %bitcast.133, f32[2,512,512,8]{2,1,3,0:T(8,128)S(1)} %get-tuple-element.227, pred[512,512]{0,1:T(8,128)(4,1)S(1)} %broadcast_compare_fusion), kind=kLoop, calls=%fused_computation.1 | loop fusion | flops 29351936 | bytes 17104896 | tf_op jit(solution)/shard_map/while/body/eval_jaxpr/cond/branch_1_fun/reduce_sum | solution.py:32
  305.2 8.7 %bitcast_add_fusion = f32[2,1,8,512,128]{4,3,2,0,1:T(8,128)} fusion(f32[2,1,8,512,128]{4,3,2,0,1:T(8,128)} %get-tuple-element.142, f32[2,8,512]{2,1,0:T(8,128)S(1)} %get-tuple-element.224, bf16[2,4096,128]{2,1,0:T(8,128)(2,1)} %get-tuple-element.143, s32[]{:T(128)S(6)} %select_n.28, f32[2,512,512,8]{2,1,3,0:T(8,128)S(1)} %get-tuple-element.227, ...), kind=kOutput, calls=%fused_computation.6 | convolution fusion | flops 1096810496 | bytes 25755652 | tf_op jit(solution)/shard_map/while/body/eval_jaxpr/cond/branch_1_fun/pkgqn,pnkd->pkgqd/dot_general | solution.py:33
  315.0 16.9 %conditional.2 = ((f32[2,1,8,512]{3,2,0,1:T(8,128)S(1)}, f32[2,1,8,512]{3,2,0,1:T(8,128)S(1)}, f32[2,1,8,512,128]{4,3,2,0,1:T(8,128)})) conditional(s32[]{:T(128)} %convert_element_type.84, (f32[2,1,8,512]{3,2,0,1:T(8,128)S(1)}, f32[2,1,8,512]{3,2,0,1:T(8,128)S(1)}, f32[2,1,8,512,128]{4,3,2,0,1:T(8,128)}) %tuple.50, (s32[]{:T(128)}, s32[]{:T(128)}, ...), branch_computations={%region_1.1_spmd, %region_2.4_spmd} | conditional | flops 2212783104 | bytes 62922836 | solution.py:55
  315.3 3.9 fusion
  319.2 4.0 %convert_reduce_fusion = f32[2,8,512]{2,1,0:T(8,128)S(1)} fusion(f32[2,8,512]{2,1,0:T(8,128)S(1)} %bitcast.133, f32[2,512,512,8]{2,1,3,0:T(8,128)S(1)} %get-tuple-element.227, pred[512,512]{0,1:T(8,128)(4,1)S(1)} %broadcast_compare_fusion), kind=kLoop, calls=%fused_computation.1 | loop fusion | flops 29351936 | bytes 17104896 | tf_op jit(solution)/shard_map/while/body/eval_jaxpr/cond/branch_1_fun/reduce_sum | solution.py:32
  323.3 8.7 %bitcast_add_fusion = f32[2,1,8,512,128]{4,3,2,0,1:T(8,128)} fusion(f32[2,1,8,512,128]{4,3,2,0,1:T(8,128)} %get-tuple-element.142, f32[2,8,512]{2,1,0:T(8,128)S(1)} %get-tuple-element.224, bf16[2,4096,128]{2,1,0:T(8,128)(2,1)} %get-tuple-element.143, s32[]{:T(128)S(6)} %select_n.28, f32[2,512,512,8]{2,1,3,0:T(8,128)S(1)} %get-tuple-element.227, ...), kind=kOutput, calls=%fused_computation.6 | convolution fusion | flops 1096810496 | bytes 25755652 | tf_op jit(solution)/shard_map/while/body/eval_jaxpr/cond/branch_1_fun/pkgqn,pnkd->pkgqd/dot_general | solution.py:33
  333.1 16.9 %conditional.2 = ((f32[2,1,8,512]{3,2,0,1:T(8,128)S(1)}, f32[2,1,8,512]{3,2,0,1:T(8,128)S(1)}, f32[2,1,8,512,128]{4,3,2,0,1:T(8,128)})) conditional(s32[]{:T(128)} %convert_element_type.84, (f32[2,1,8,512]{3,2,0,1:T(8,128)S(1)}, f32[2,1,8,512]{3,2,0,1:T(8,128)S(1)}, f32[2,1,8,512,128]{4,3,2,0,1:T(8,128)}) %tuple.50, (s32[]{:T(128)}, s32[]{:T(128)}, ...), branch_computations={%region_1.1_spmd, %region_2.4_spmd} | conditional | flops 2212783104 | bytes 62922836 | solution.py:55
  333.3 3.9 fusion
  337.3 4.0 %convert_reduce_fusion = f32[2,8,512]{2,1,0:T(8,128)S(1)} fusion(f32[2,8,512]{2,1,0:T(8,128)S(1)} %bitcast.133, f32[2,512,512,8]{2,1,3,0:T(8,128)S(1)} %get-tuple-element.227, pred[512,512]{0,1:T(8,128)(4,1)S(1)} %broadcast_compare_fusion), kind=kLoop, calls=%fused_computation.1 | loop fusion | flops 29351936 | bytes 17104896 | tf_op jit(solution)/shard_map/while/body/eval_jaxpr/cond/branch_1_fun/reduce_sum | solution.py:32
  341.3 8.7 %bitcast_add_fusion = f32[2,1,8,512,128]{4,3,2,0,1:T(8,128)} fusion(f32[2,1,8,512,128]{4,3,2,0,1:T(8,128)} %get-tuple-element.142, f32[2,8,512]{2,1,0:T(8,128)S(1)} %get-tuple-element.224, bf16[2,4096,128]{2,1,0:T(8,128)(2,1)} %get-tuple-element.143, s32[]{:T(128)S(6)} %select_n.28, f32[2,512,512,8]{2,1,3,0:T(8,128)S(1)} %get-tuple-element.227, ...), kind=kOutput, calls=%fused_computation.6 | convolution fusion | flops 1096810496 | bytes 25755652 | tf_op jit(solution)/shard_map/while/body/eval_jaxpr/cond/branch_1_fun/pkgqn,pnkd->pkgqd/dot_general | solution.py:33
  350.0 2.9 fusion.21
  356.5 8.3 %reduce_sum.41 = bf16[8,2,512,256]{3,2,1,0:T(8,128)(2,1)} reduce(bf16[2,8,2,512,256]{4,3,2,1,0:T(8,128)(2,1)} %bitcast.20, bf16[]{:T(256)} %constant.76.clone.1), dimensions={0}, to_apply=%region_7.8 | reduce | flops 2097152 | bytes 12582914 | tf_op jit(solution)/shard_map/reduce_sum | solution.py:128
  364.7 2.5 copy.66
  369.2 4.6 %fusion.17 = (f32[32,8]{0,1:T(8,128)S(1)}, f32[2,4096,32,8]{1,2,3,0:T(8,128)}) fusion(pred[32,2]{0,1:T(4,128)(4,1)S(1)} %iota_compare_fusion.1, bf16[2,4096,256]{2,1,0:T(8,128)(2,1)S(1)} %bitcast.136, bf16[32,1024]{1,0:T(8,128)(2,1)S(1)} %copy-done.4), kind=kOutput, calls=%fused_computation.28 | convolution fusion | flops 543162112 | bytes 10552832 | tf_op jit(solution)/shard_map/rkgd,tnkd->rkgtn/dot_general | solution.py:135
  373.9 5.0 %convert_reduce_fusion.1 = (f32[32,8]{0,1:T(8,128)S(1)}, bf16[32,8,2,4096]{3,0,1,2:T(8,128)(2,1)S(1)}) fusion(f32[32,8]{0,1:T(8,128)S(1)} %max.19, f32[2,4096,32,8]{1,2,3,0:T(8,128)} %get-tuple-element.235, pred[32,2]{0,1:T(4,128)(4,1)S(1)} %iota_compare_fusion.1), kind=kLoop, calls=%fused_computation.26 | loop fusion | flops 14679808 | bytes 12585024 | tf_op jit(solution)/shard_map/reduce_sum | solution.py:151
  378.9 2.4 fusion.25
  381.8 4.7 %fusion.28 = bf16[32,1,8,128]{3,2,0,1:T(8,128)(2,1)S(1)} fusion(f32[32,1,8,128]{3,2,0,1:T(8,128)S(1)} %fusion.25, bf16[32,1024,128]{2,1,0:T(8,128)(2,1)} %param.18, f32[32,8]{1,0:T(8,128)S(1)} %add.70, f32[32,8,1024]{2,1,0:T(8,128)S(1)} %copy-done, f32[32,8]{1,0:T(8,128)S(1)} %copy.69, pred[32,1024]{1,0:T(8,128)(4,1)S(1)} %iota_compare_fusion), kind=kOutput, calls=%fused_computation.43 | convolution fusion | flops 67993600 | bytes 9668608 | tf_op jit(solution)/shard_map/rkgn,rnkd->rkgd/dot_general | solution.py:154
  (86 shorter events, 20.1 us)
Async XLA Ops:
  7.2 138.6 %all-gather.3.cloned.1.call-start = ((), (), s32[]{:S(2)}) async-start(), calls=%async_computation.1 | async-start | bytes 2359296 | tf_op jit(solution)/shard_map/all_gather | solution.py:94
  25.8 8.1 %copy-start.3 = (bf16[2,512,1024]{2,1,0:T(8,128)(2,1)S(1)}, bf16[2,512,1024]{2,1,0:T(8,128)(2,1)}, u32[]{:S(2)}) copy-start(bf16[2,512,1024]{2,1,0:T(8,128)(2,1)} %param.13) | copy-start | bytes 6291460
  25.8 330.7 %all-to-all-start = ((bf16[16,2,512,256]{3,2,1,0:T(8,128)(2,1)}), bf16[16,2,512,256]{3,2,1,0:T(8,128)(2,1)}, u32[]{:S(2)}, u32[]{:S(2)}) async-start(bf16[16,2,512,256]{3,2,1,0:T(8,128)(2,1)} %copy.64), calls=%async_computation | async-start | bytes 16777216 | tf_op jit(solution)/shard_map/all_to_all | solution.py:123
  33.1 6.4 %copy-start.4 = (bf16[32,1024]{1,0:T(8,128)(2,1)S(1)}, bf16[32,1024]{1,0:T(8,128)(2,1)}, u32[]{:S(2)}) copy-start(bf16[32,1024]{1,0:T(8,128)(2,1)} %param.16) | copy-start | bytes 196612
  33.2 6.4 %copy-start.5 = (s32[32]{0:T(128)S(1)}, s32[32]{0:T(128)}, u32[]{:S(2)}) copy-start(s32[32]{0:T(128)} %param.19) | copy-start | bytes 388
  33.2 169.9 %all-gather.5.cloned.1.call-start = ((), (), s32[]{:S(2)}) async-start(), calls=%async_computation.2 | async-start | bytes 2359296 | tf_op jit(solution)/shard_map/all_gather | solution.py:95
  33.9 12.5 %copy-start.6 = (s32[32]{0:T(128)S(1)}, s32[32]{0:T(128)}, u32[]{:S(2)}) copy-start(s32[32]{0:T(128)} %param.21) | copy-start | bytes 388
  367.2 1.9 copy-start.1
  373.9 5.0 %copy-start.2 = (bf16[2,8,512,256]{3,2,1,0:T(8,128)(2,1)S(1)}, bf16[2,8,512,256]{3,2,1,0:T(8,128)(2,1)}, u32[]{:S(2)}) copy-start(bf16[2,8,512,256]{3,2,1,0:T(8,128)(2,1)} %copy-done.1) | copy-start | bytes 12582916
  378.9 2.5 copy-start
Sparse Core Ops, SparseCore 0:
  10.3 135.3 all-gather.2
  148.1 54.9 all-gather.4
where the time goes:
time: 396 us; the launch traced here: 394 us
  waiting for transfers between devices  158 us (40%)
  matrix products  125 us (32%)
  other arithmetic  50.8 us (13%)
  local copies, waits for them, and re-layouts  33.7 us (9%)
  between operations  14.2 us (4%)
  starting transfers between devices  7.59 us (2%)
  loops' own time  5.17 us (1%)
    all_gather x1, waiting for transfers between devices, on_device(): lax.all_gather(prompt_key, 'ctx', axis=1, tiled=True)  99.3 us
    dot_general x8, matrix products, attend_block(): jnp.einsum('pkgqn,pnkd->pkgqd', weights, value_block, preferred_element_t...  69.3 us
    all_gather x1, waiting for transfers between devices, on_device(): lax.all_gather(prompt_value, 'ctx', axis=1, tiled=True)  57.4 us
    reduce_sum x8, other arithmetic, attend_block(): totals = totals * factor + jnp.sum(weights, axis=-1, dtype=jnp.float32)  32 us
    dot_general x8, matrix products, attend_block(): jnp.einsum('pqkgd,pnkd->pkgqn', queries, key_block, preferred_element_typ...  31.2 us
    convert_element_type x1, local copies, waits for them, and re-layouts, on_device(): outgoing = jnp.einsum('oti,isc->otsc', picked, local_pairs, preferred_ele...  9.61 us
    reduce_sum x1, other arithmetic, on_device(): merged = jnp.sum(incoming, axis=0)  8.25 us
  transfers between devices with their start and end apart: 3, of which 2 were waited for; matrix products, arithmetic and copies ran while one was open for 45% of the time, Pallas kernels for 0%

commit v1 on v0

v1 whole, which is shorter than its diff:
```python
import jax
import jax.numpy as jnp
from jax import lax
from jax.experimental import pallas as pl
from jax.experimental.pallas import tpu as pltpu
from jax.sharding import PartitionSpec as P

HEADS = 64
KV_HEADS = 8
HEAD_DIM = 128
GROUP = HEADS // KV_HEADS
FLOOR = -1e30
SCALE2 = 1.4426950408889634 / HEAD_DIM**0.5
MESH = pl.DeviceIdType.MESH
CTX = 8
XS = 4
BLOCK = 512
REQS = 32
MAXC = 1024
CACHE_GROUP = 8
AUG = HEAD_DIM + 16

N_SENDS = 6 + 2 + 4 + 2 + 16


def dot_t(a, b):
    return lax.dot_general(a, b, (((1,), (1,)), ((), ())), preferred_element_type=jnp.float32)


def dot(a, b):
    return lax.dot_general(a, b, (((1,), (0,)), ((), ())), preferred_element_type=jnp.float32)


def split_scaled(q):
    scaled = q.astype(jnp.float32) * SCALE2
    high = scaled.astype(jnp.bfloat16)
    low = (scaled - high.astype(jnp.float32)).astype(jnp.bfloat16)
    return jnp.concatenate([high, low], axis=1)


def twice(k):
    return jnp.concatenate([k, k], axis=1)


def with_ones(v):
    return jnp.concatenate([v.T, jnp.ones((AUG - HEAD_DIM, v.shape[0]), v.dtype)], axis=0)


def kernel(
    pq, pk, pv, sq, ck, cv, lengths, owner_slots, request_slot,
    out, step_out,
    kv, q_in, q_split, acc, top, out_v, cache_k, cache_v, sq_in, sq_rows,
    c_out, c_top, c_sum, p_acc, p_top, step_v,
    send_sem, recv_sem, sib_sem, in_sem, cache_sem, out_sem,
):
    section = lax.axis_index("section")
    me = lax.axis_index("ctx")
    y, x = me // XS, lax.rem(me, XS)
    first = section * 2

    def at(row, col):
        return row * XS + lax.rem(col + XS, XS)

    left, right = at(y, x - 1), at(y, x + 1)
    across, opposite = at(1 - y, x), at(y, x + 2)
    far_left, far_right, far_opposite = at(1 - y, x - 1), at(1 - y, x + 1), at(1 - y, x + 2)
    owner = section * CTX + me

    loads = [
        pltpu.make_async_copy(pk, kv.at[0, pl.ds(first, 2), me], in_sem.at[0]),
        pltpu.make_async_copy(pv, kv.at[1, pl.ds(first, 2), me], in_sem.at[1]),
        pltpu.make_async_copy(sq, sq_in, in_sem.at[2]),
        pltpu.make_async_copy(pq, q_in, in_sem.at[3]),
    ]
    for load in loads:
        load.start()

    def cache_copies(g):
        rows = pl.ds(g * CACHE_GROUP, CACHE_GROUP)
        return (
            pltpu.make_async_copy(ck.at[rows], cache_k.at[rows], cache_sem.at[0, g]),
            pltpu.make_async_copy(cv.at[rows], cache_v.at[rows], cache_sem.at[1, g]),
        )

    for g in range(REQS // CACHE_GROUP):
        for copy in cache_copies(g):
            copy.start()

    barrier = pltpu.get_barrier_semaphore()
    for peer in (left, right, across):
        pl.semaphore_signal(barrier, inc=1, device_id={"ctx": peer}, device_id_type=MESH)
    pl.semaphore_signal(barrier, inc=1, device_id={"section": 1 - section}, device_id_type=MESH)
    pl.semaphore_wait(barrier, 4)

    def block_of(part, j):
        return kv.at[part, pl.ds(first, 2), j]

    def move(slot, part, j, to, src=None):
        return pltpu.make_async_remote_copy(
            src_ref=block_of(part, j) if src is None else src,
            dst_ref=block_of(part, j),
            send_sem=send_sem.at[slot],
            recv_sem=recv_sem.at[part, j],
            device_id={"ctx": to},
            device_id_type=MESH,
        )

    def share(slot, part, j, src=None):
        return pltpu.make_async_remote_copy(
            src_ref=block_of(part, j) if src is None else src,
            dst_ref=block_of(part, j),
            send_sem=send_sem.at[slot],
            recv_sem=sib_sem.at[part, j],
            device_id={"section": 1 - section},
            device_id_type=MESH,
        )

    def shared(part, j):
        other = kv.at[part, pl.ds(2 - first, 2), j]
        return pltpu.make_async_remote_copy(
            src_ref=other, dst_ref=other, send_sem=send_sem.at[0], recv_sem=sib_sem.at[part, j],
            device_id={"section": 1 - section}, device_id_type=MESH,
        )

    def send(copy):
        copy.start()

    for part, src in ((0, pk), (1, pv)):
        for n, to in enumerate((left, right, across)):
            send(move(part * 3 + n, part, me, to, src))
    send(share(14, 0, me, pk))
    send(share(15, 1, me, pv))

    def arrive(part, j):
        move(0, part, j, me).wait_recv()

    loads[3].wait()

    def split_step(n, _):
        p, h = n // GROUP, lax.rem(n, GROUP)
        cols = pl.ds(pl.multiple_of(h * HEAD_DIM, HEAD_DIM), HEAD_DIM)
        q_split[p, h] = split_scaled(q_in[p, :, cols])
        return 0

    lax.fori_loop(0, 2 * GROUP, split_step, 0)

    loads[2].wait()
    for h in range(GROUP):
        sq_rows[:, h, :] = sq_in[:, h * HEAD_DIM : (h + 1) * HEAD_DIM].astype(jnp.float32)

    def cache_step(g, _):
        for copy in cache_copies(g):
            copy.wait()
        scores = []
        for u in range(CACHE_GROUP):
            r = g * CACHE_GROUP + u
            scores.append(dot_t(sq_rows[r].astype(jnp.bfloat16), cache_k[r]))
        for u in range(CACHE_GROUP):
            r = g * CACHE_GROUP + u
            column = lax.broadcasted_iota(jnp.int32, (GROUP, MAXC), 1)
            s = jnp.where(column < lengths[r], scores[u], FLOOR)
            highest = jnp.max(s, axis=1, keepdims=True)
            w = jnp.exp2((s - highest) * SCALE2).astype(jnp.bfloat16)
            total = jnp.sum(w.astype(jnp.float32), axis=1, keepdims=True)
            c_out[r] = dot(w, cache_v[r])
            c_top[r] = jnp.broadcast_to(highest * SCALE2, (GROUP, HEAD_DIM))
            c_sum[r] = jnp.broadcast_to(total, (GROUP, HEAD_DIM))
        return 0

    lax.fori_loop(0, REQS // CACHE_GROUP, cache_step, 0)

    for part in (0, 1):
        loads[part].wait()
    for n, j in enumerate((left, right, across)):
        arrive(0, j)
    send(move(6, 0, left, right))
    send(move(8, 0, across, left))
    send(move(9, 0, across, right))
    for n, j in enumerate((left, right, across)):
        send(share(16 + n, 0, j))

    def diagonal_step(p, _):
        keys = twice(kv[0, first + p, me])
        values = with_ones(kv[1, first + p, me])
        key_at = lax.broadcasted_iota(jnp.int32, (BLOCK, BLOCK), 0)
        query_at = lax.broadcasted_iota(jnp.int32, (BLOCK, BLOCK), 1)
        scores = [dot_t(keys, q_split[p, h]) for h in range(GROUP)]
        for h in range(GROUP):
            s = jnp.where(key_at <= query_at, scores[h], FLOOR)
            highest = jnp.max(s, axis=0, keepdims=True)
            w = jnp.exp2(s - highest).astype(jnp.bfloat16)
            acc[p, h] = dot(values, w)
            top[p, h : h + 1, :] = highest
        return 0

    lax.fori_loop(0, 2, diagonal_step, 0)

    for j in (left, right, across):
        arrive(1, j)
    send(move(7, 1, right, left))
    send(move(10, 1, across, left))
    send(move(11, 1, across, right))
    for n, j in enumerate((left, right, across)):
        send(share(19 + n, 1, j))

    order = (left, right, across, opposite, far_left, far_right, far_opposite)

    def main_step(n, _):
        k, p = n // 2, lax.rem(n, 2)

        @pl.when(n == 2)
        def _():
            for part in (0, 1):
                arrive(part, opposite)
                send(move(12 + part, part, opposite, across))
                send(share(22 + part, part, opposite))

        @pl.when(n == 8)
        def _():
            for m, j in enumerate((far_left, far_right)):
                for part in (0, 1):
                    arrive(part, j)
                    send(share(24 + 2 * m + part, part, j))

        @pl.when(n == 12)
        def _():
            for part in (0, 1):
                arrive(part, far_opposite)
                send(share(28 + part, part, far_opposite))

        j = order[0]
        for m in range(1, len(order)):
            j = jnp.where(k == m, order[m], j)

        @pl.when(j < me)
        def _():
            keys = twice(kv[0, first + p, j])
            values = with_ones(kv[1, first + p, j])
            scores = [dot_t(keys, q_split[p, h]) for h in range(GROUP)]
            for h in range(GROUP):
                s = scores[h]
                before = top[p, h : h + 1, :]
                highest = jnp.maximum(before, jnp.max(s, axis=0, keepdims=True))
                w = jnp.exp2(s - highest).astype(jnp.bfloat16)
                acc[p, h] = acc[p, h] * jnp.exp2(before - highest) + dot(values, w)
                top[p, h : h + 1, :] = highest

        return 0

    lax.fori_loop(0, 2 * len(order), main_step, 0)

    def finish_step(n, _):
        p, h = n // GROUP, lax.rem(n, GROUP)
        a = acc[p, h]
        cols = pl.ds(pl.multiple_of(h * HEAD_DIM, HEAD_DIM), HEAD_DIM)
        out_v[p, :, cols] = (a[:HEAD_DIM] / a[HEAD_DIM : HEAD_DIM + 1]).T.astype(jnp.bfloat16)
        return 0

    lax.fori_loop(0, 2 * GROUP, finish_step, 0)
    out_copy = pltpu.make_async_copy(out_v, out, out_sem.at[0])
    out_copy.start()

    for part in (0, 1):
        for j in range(CTX):
            shared(part, j).wait_recv()
    step_q = jnp.concatenate(
        [split_scaled(sq_in[:, h * HEAD_DIM : (h + 1) * HEAD_DIM]) for h in range(GROUP)], axis=0
    )
    width = GROUP * REQS
    request = lax.rem(lax.broadcasted_iota(jnp.int32, (1, width), 1), REQS)
    slot = jnp.zeros((1, width), jnp.int32)
    for r in range(REQS):
        slot = jnp.where(request == r, request_slot[r], slot)
    second = slot == 1
    in_second = second.astype(jnp.bfloat16)
    in_first = (1.0 - second.astype(jnp.float32)).astype(jnp.bfloat16)
    prompts = (owner_slots[owner, 0], owner_slots[owner, 1])
    p_acc[...] = jnp.zeros_like(p_acc)
    p_top[...] = jnp.full(p_top.shape, FLOOR, jnp.float32)

    def persona_step(i, _):
        scores = []
        for u in range(2):
            j = i * 2 + u
            a = dot_t(twice(kv[0, prompts[0], j]), step_q)
            b = dot_t(twice(kv[0, prompts[1], j]), step_q)
            scores.append(jnp.where(second, b, a))
        before = p_top[0:1, :]
        highest = before
        for s in scores:
            highest = jnp.maximum(highest, jnp.max(s, axis=0, keepdims=True))
        total = p_acc[...] * jnp.exp2(before - highest)
        for u in range(2):
            j = i * 2 + u
            w = jnp.exp2(scores[u] - highest).astype(jnp.bfloat16)
            total = total + dot(with_ones(kv[1, prompts[0], j]), w * in_first)
            total = total + dot(with_ones(kv[1, prompts[1], j]), w * in_second)
        p_acc[...] = total
        p_top[0:1, :] = highest
        return 0

    lax.fori_loop(0, CTX // 2, persona_step, 0)

    def rows(ref):
        return jnp.concatenate([ref[:, h, :] for h in range(GROUP)], axis=0)

    def spread(row):
        return jnp.broadcast_to(row, (HEAD_DIM, width)).T

    total_p, top_p = spread(p_acc[HEAD_DIM : HEAD_DIM + 1, :]), spread(p_top[0:1, :])
    top_c = rows(c_top)
    highest = jnp.maximum(top_p, top_c)
    weight_p, weight_c = jnp.exp2(top_p - highest), jnp.exp2(top_c - highest)
    mixed = p_acc[:HEAD_DIM, :].T * weight_p + rows(c_out) * weight_c
    mixed = mixed / (total_p * weight_p + rows(c_sum) * weight_c)
    for h in range(GROUP):
        step_v[:, h * HEAD_DIM : (h + 1) * HEAD_DIM] = mixed[h * REQS : (h + 1) * REQS].astype(
            jnp.bfloat16
        )
    step_copy = pltpu.make_async_copy(step_v, step_out, out_sem.at[1])
    step_copy.start()

    for sent in range(N_SENDS):
        move(sent, 0, me, left).wait_send()
    out_copy.wait()
    step_copy.wait()


def on_device(pq, pk, pv, sq, ck, cv, lengths, owner_slots, request_slot):
    anywhere = pl.BlockSpec(memory_space=pl.ANY)
    scalars = pl.BlockSpec(memory_space=pltpu.SMEM)
    f32, bf16 = jnp.float32, jnp.bfloat16
    return pl.pallas_call(
        kernel,
        out_shape=(
            jax.ShapeDtypeStruct(pq.shape, bf16),
            jax.ShapeDtypeStruct(sq.shape, bf16),
        ),
        in_specs=[anywhere] * 6 + [scalars] * 3,
        out_specs=(anywhere, anywhere),
        scratch_shapes=[
            pltpu.VMEM((2, 4, CTX, BLOCK, HEAD_DIM), bf16),
            pltpu.VMEM(pq.shape, bf16),
            pltpu.VMEM((2, GROUP, BLOCK, 2 * HEAD_DIM), bf16),
            pltpu.VMEM((2, GROUP, AUG, BLOCK), f32),
            pltpu.VMEM((2, GROUP, BLOCK), f32),
            pltpu.VMEM(pq.shape, bf16),
            pltpu.VMEM(ck.shape, bf16),
            pltpu.VMEM(cv.shape, bf16),
            pltpu.VMEM(sq.shape, bf16),
            pltpu.VMEM((REQS, GROUP, HEAD_DIM), f32),
            pltpu.VMEM((REQS, GROUP, HEAD_DIM), f32),
            pltpu.VMEM((REQS, GROUP, HEAD_DIM), f32),
            pltpu.VMEM((REQS, GROUP, HEAD_DIM), f32),
            pltpu.VMEM((AUG, GROUP * REQS), f32),
            pltpu.VMEM((8, GROUP * REQS), f32),
            pltpu.VMEM(sq.shape, bf16),
            pltpu.SemaphoreType.DMA((N_SENDS,)),
            pltpu.SemaphoreType.DMA((2, CTX)),
            pltpu.SemaphoreType.DMA((2, CTX)),
            pltpu.SemaphoreType.DMA((4,)),
            pltpu.SemaphoreType.DMA((2, REQS // CACHE_GROUP)),
            pltpu.SemaphoreType.DMA((2,)),
        ],
        compiler_params=pltpu.CompilerParams(
            collective_id=0, has_side_effects=True, vmem_limit_bytes=60 << 20
        ),
        cost_estimate=pl.CostEstimate(
            flops=18_000_000_000, bytes_accessed=24 << 20, transcendentals=34_000_000
        ),
        name="prompt_and_step",
    )(pq, pk, pv, sq, ck, cv, lengths, owner_slots, request_slot)


def solution(mesh):
    in_specs = (
        P("section", "ctx", "head"),
        P("section", "ctx", "head"),
        P("section", "ctx", "head"),
        P(("section", "ctx"), "head"),
        P(("section", "ctx"), None, "head"),
        P(("section", "ctx"), None, "head"),
        P(("section", "ctx")),
        P(),
        P(("section", "ctx")),
    )
    out_specs = (P("section", "ctx", "head"), P(("section", "ctx"), "head"))
    return jax.shard_map(
        on_device, mesh=mesh, in_specs=in_specs, out_specs=out_specs, check_vma=False
    )
```

time: 396 us -> 75 us (0.19)
  waiting for transfers between devices: 158 us -> 0 us
  matrix products: 125 us -> 0 us
  Pallas kernels: 0 us -> 69.1 us
  other arithmetic: 50.8 us -> 0 us
  local copies, waits for them, and re-layouts: 33.7 us -> 5.1 us
  between operations: 14.2 us -> 0.65 us
  starting transfers between devices: 7.59 us -> 0 us
  loops' own time: 5.17 us -> 0 us
    all_gather x2 -> x0, waiting for transfers between devices: 157 us -> none  [the longest x1 99.3 us: on_device(): lax.all_gather(prompt_key, 'ctx', axis=1, tiled=True)]
    dot_general x21 -> x0, matrix products: 125 us -> none  [the longest x8 69.3 us: attend_block(): jnp.einsum('pkgqn,pnkd->pkgqd', weights, value_block, preferred_element_t...]
    pallas_call x0 -> x1, Pallas kernels: none -> 69.1 us  [on_device(): pl.pallas_call(kernel, out_shape=(jax.ShapeDtypeStruct(pq.shape, bf16), j...]
    reduce_sum x11 -> x0, other arithmetic: 45.7 us -> none  [the longest x8 32 us: attend_block(): totals = totals * factor + jnp.sum(weights, axis=-1, dtype=jnp.float32)]
    convert_element_type x3 -> x0, local copies, waits for them, and re-layouts: 13.3 us -> none  [the longest x1 9.61 us: on_device(): outgoing = jnp.einsum('oti,isc->otsc', picked, local_pairs, preferred_ele...]
    all_to_all x1 -> x0, starting transfers between devices: 7.33 us -> none  [on_device(): lax.all_to_all(outgoing, ('section', 'ctx'), split_axis=0, concat_axis=0,...]
    another operation x9 -> x0, loops' own time: 5.17 us -> none  [the longest x1 4.57 us: prompt_attend(): lax.scan(advance, running, jnp.arange(key_rows // block_rows, dtype=jnp.i...]
    dynamic_slice x8 -> x0, local copies, waits for them, and re-layouts: 4.66 us -> none  [prompt_attend(): lax.scan(advance, running, jnp.arange(key_rows // block_rows, dtype=jnp.i...]
  transfers between devices with their start and end apart: 3 -> 0, of which waited for: 2 -> 0; matrix products, arithmetic and copies ran while one was open for 45% -> 0% of each run, Pallas kernels for 0% -> 0%
where the time goes in v1:
time: 75 us; the launch traced here: 74.8 us
  Pallas kernels  69.1 us (92%)
  local copies, waits for them, and re-layouts  5.1 us (7%)
    pallas_call x1, Pallas kernels, on_device(): pl.pallas_call(kernel, out_shape=(jax.ShapeDtypeStruct(pq.shape, bf16), j...  69.1 us
    unnamed x5, local copies, waits for them, and re-layouts  5.1 us

profile of v1, /device:TPU:30, one launch (start us, length us, event | category | flops | bytes accessed | tf_op | source)
XLA Modules:
  0.0 74.8 jit_solution(12209971287241138713)
XLA Ops:
  0.6 1.4 %copy.11.owner_slots = s32[16,2]{1,0:T(8,128)} copy(s32[16,2]{0,1:T(2,128)} %param.16) | data formatting | bytes 256 | tf_op args[7]
  2.0 69.1 %prompt_and_step.1 = (bf16[2,512,1024]{2,1,0:T(8,128)(2,1)}, bf16[32,1024]{1,0:T(8,128)(2,1)}) custom-call(bf16[2,512,1024]{2,1,0:T(8,128)(2,1)} %pq.1, bf16[2,512,128]{2,1,0:T(8,128)(2,1)} %pk.1, bf16[2,512,128]{2,1,0:T(8,128)(2,1)} %pv.1, bf16[32,1024]{1,0:T(8,128)(2,1)} %sq.1, bf16[32,1024,128]{2,1,0:T(8,128)(2,1)} %ck.1, bf16[32,1024,128]{2,1,0:T(8,128)(2,1)} %cv.1, ...), custom_call_target="tpu_custom_call" | custom-call | flops 17999998976 | bytes 25165824 | tf_op jit(solution)/shard_map/prompt_and_step/pallas_call | solution.py:333
  71.1 0.0 copy-start
  71.1 3.1 %copy.14 = bf16[2,512,1024]{2,1,0:T(8,128)(2,1)} copy(bf16[2,512,1024]{2,1,0:T(8,128)(2,1)} %get-tuple-element.4) | data formatting | bytes 4194304
  74.2 0.0 copy-done
  74.2 0.6 copy.15
Async XLA Ops:
  71.1 3.1 %copy-start = (bf16[32,1024]{1,0:T(8,128)(2,1)S(1)}, bf16[32,1024]{1,0:T(8,128)(2,1)}, u32[]{:S(2)}) copy-start(bf16[32,1024]{1,0:T(8,128)(2,1)} %get-tuple-element.5) | copy-start | bytes 196612

commit v2 on v1

v2 whole, which is shorter than its diff:
```python
import jax
import jax.numpy as jnp
from jax import lax
from jax.experimental import pallas as pl
from jax.experimental.pallas import tpu as pltpu
from jax.sharding import PartitionSpec as P

HEADS = 64
KV_HEADS = 8
HEAD_DIM = 128
GROUP = HEADS // KV_HEADS
FLOOR = -1e30
SCALE2 = 1.4426950408889634 / HEAD_DIM**0.5
MESH = pl.DeviceIdType.MESH
CTX = 8
XS = 4
BLOCK = 512
REQS = 32
MAXC = 1024
CACHE_GROUP = 8
AUG = HEAD_DIM + 16

HALF = GROUP // 2
PARTNER = CTX // 2

N_SENDS = 6 + 2 + 4 + 2 + 16


def dot_t(a, b):
    return lax.dot_general(a, b, (((1,), (1,)), ((), ())), preferred_element_type=jnp.float32)


def dot(a, b):
    return lax.dot_general(a, b, (((1,), (0,)), ((), ())), preferred_element_type=jnp.float32)


def split_scaled(q):
    scaled = q.astype(jnp.float32) * SCALE2
    high = scaled.astype(jnp.bfloat16)
    low = (scaled - high.astype(jnp.float32)).astype(jnp.bfloat16)
    return jnp.concatenate([high, low], axis=1)


def twice(k):
    return jnp.concatenate([k, k], axis=1)


def with_ones(v):
    return jnp.concatenate([v.T, jnp.ones((AUG - HEAD_DIM, v.shape[0]), v.dtype)], axis=0)


def kernel(
    pq, pk, pv, sq, ck, cv, lengths, owner_slots, request_slot,
    out, step_out,
    kv, q_in, q_far, q_split, acc, top, out_v, out_far, cache_k, cache_v, sq_in, sq_rows,
    c_out, c_top, c_sum, p_acc, p_top, step_v,
    send_sem, recv_sem, sib_sem, far_sem, in_sem, cache_sem, out_sem,
):
    section = lax.axis_index("section")
    me = lax.axis_index("ctx")
    y, x = me // XS, lax.rem(me, XS)
    first = section * 2
    heavy = me >= PARTNER

    def at(row, col):
        return row * XS + lax.rem(col + XS, XS)

    left, right = at(y, x - 1), at(y, x + 1)
    across, opposite = at(1 - y, x), at(y, x + 2)
    far_left, far_right, far_opposite = at(1 - y, x - 1), at(1 - y, x + 1), at(1 - y, x + 2)
    owner = section * CTX + me

    loads = []
    for p in (0, 1):
        for part, src in ((0, pk), (1, pv)):
            loads.append(
                pltpu.make_async_copy(src.at[p], kv.at[first + p, me, part], in_sem.at[len(loads)])
            )
    loads.append(pltpu.make_async_copy(pq, q_in, in_sem.at[4]))
    loads.append(pltpu.make_async_copy(sq, sq_in, in_sem.at[5]))
    for load in loads:
        load.start()

    def cache_copies(g):
        rows = pl.ds(g * CACHE_GROUP, CACHE_GROUP)
        return (
            pltpu.make_async_copy(ck.at[rows], cache_k.at[rows], cache_sem.at[0, g]),
            pltpu.make_async_copy(cv.at[rows], cache_v.at[rows], cache_sem.at[1, g]),
        )

    for g in range(REQS // CACHE_GROUP):
        for copy in cache_copies(g):
            copy.start()

    barrier = pltpu.get_barrier_semaphore()
    for peer in (left, right, across):
        pl.semaphore_signal(barrier, inc=1, device_id={"ctx": peer}, device_id_type=MESH)
    pl.semaphore_signal(barrier, inc=1, device_id={"section": 1 - section}, device_id_type=MESH)
    pl.semaphore_wait(barrier, 4)

    def move(slot, p, j, to):
        return pltpu.make_async_remote_copy(
            src_ref=kv.at[first + p, j],
            dst_ref=kv.at[first + p, j],
            send_sem=send_sem.at[slot],
            recv_sem=recv_sem.at[p, j],
            device_id={"ctx": to},
            device_id_type=MESH,
        )

    def share(n, p, j):
        return pltpu.make_async_remote_copy(
            src_ref=kv.at[first + p, j],
            dst_ref=kv.at[first + p, j],
            send_sem=send_sem.at[14 + 2 * n + p],
            recv_sem=sib_sem.at[p, j],
            device_id={"section": 1 - section},
            device_id_type=MESH,
        )

    def shared(p, j):
        other = kv.at[2 - first + p, j]
        return pltpu.make_async_remote_copy(
            src_ref=other, dst_ref=other, send_sem=send_sem.at[0], recv_sem=sib_sem.at[p, j],
            device_id={"section": 1 - section}, device_id_type=MESH,
        )

    far_cols = pl.ds(HALF * HEAD_DIM, HALF * HEAD_DIM)
    lend = pltpu.make_async_remote_copy(
        src_ref=pq.at[1, :, far_cols], dst_ref=q_far, send_sem=far_sem.at[0], recv_sem=far_sem.at[1],
        device_id={"ctx": across}, device_id_type=MESH,
    )
    give_back = pltpu.make_async_remote_copy(
        src_ref=out_far, dst_ref=out.at[1, :, far_cols], send_sem=far_sem.at[2],
        recv_sem=far_sem.at[3], device_id={"ctx": across}, device_id_type=MESH,
    )

    for p in (0, 1):
        loads[2 * p].wait()
        loads[2 * p + 1].wait()
        for n, to in enumerate((left, right, across)):
            move(p * 3 + n, p, me, to).start()

    @pl.when(heavy)
    def _():
        lend.start()

    for p in (0, 1):
        share(0, p, me).start()

    def arrive(p, j):
        move(0, p, j, me).wait_recv()

    def first_arrivals():
        for n, j in enumerate((left, right, across)):
            arrive(0, j)
        move(6, 0, left, right).start()
        move(8, 0, across, right).start()
        for n, j in enumerate((left, right, across)):
            share(1 + n, 0, j).start()

    def second_arrivals():
        for j in (left, right, across):
            arrive(1, j)
        move(7, 1, right, left).start()
        move(9, 0, across, left).start()
        move(10, 1, across, left).start()
        move(11, 1, across, right).start()
        for n, j in enumerate((left, right, across)):
            share(1 + n, 1, j).start()

    def opposite_arrives():
        for p in (0, 1):
            arrive(p, opposite)
            move(12 + p, p, opposite, across).start()
            share(4, p, opposite).start()

    def far_sides_arrive():
        for p in (0, 1):
            for n, j in enumerate((far_left, far_right)):
                arrive(p, j)
                share(5 + n, p, j).start()

    def far_opposite_arrives():
        for p in (0, 1):
            arrive(p, far_opposite)
            share(7, p, far_opposite).start()

    def split_step(n, _):
        g, u = n // HALF, lax.rem(n, HALF)
        h = lax.rem(n, GROUP)
        cols = pl.ds(pl.multiple_of(h * HEAD_DIM, HEAD_DIM), HEAD_DIM)
        q_split[g, u] = split_scaled(q_in[g // 2, :, cols])
        return 0

    loads[4].wait()
    lax.fori_loop(0, jnp.where(heavy, 3 * HALF, 4 * HALF), split_step, 0)

    def diagonal_step(p, _):
        keys = twice(kv[first + p, me, 0])
        values = with_ones(kv[first + p, me, 1])
        key_at = lax.broadcasted_iota(jnp.int32, (BLOCK, BLOCK), 0)
        query_at = lax.broadcasted_iota(jnp.int32, (BLOCK, BLOCK), 1)
        scores = [dot_t(keys, q_split[2 * p + h // HALF, h % HALF]) for h in range(GROUP)]
        for h in range(GROUP):
            g, u = 2 * p + h // HALF, h % HALF
            s = jnp.where(key_at <= query_at, scores[h], FLOOR)
            highest = jnp.max(s, axis=0, keepdims=True)
            w = jnp.exp2(s - highest).astype(jnp.bfloat16)
            acc[g, u] = dot(values, w)
            top[g, u : u + 1, :] = highest
        return 0

    lax.fori_loop(0, jnp.where(heavy, 1, 2), diagonal_step, 0)

    loads[5].wait()
    for h in range(GROUP):
        sq_rows[:, h, :] = sq_in[:, h * HEAD_DIM : (h + 1) * HEAD_DIM].astype(jnp.float32)

    def cache_step(g, _):
        @pl.when(g == 2)
        def _():
            first_arrivals()

        for copy in cache_copies(g):
            copy.wait()
        scores = []
        for u in range(CACHE_GROUP):
            r = g * CACHE_GROUP + u
            scores.append(dot_t(sq_rows[r].astype(jnp.bfloat16), cache_k[r]))
        for u in range(CACHE_GROUP):
            r = g * CACHE_GROUP + u
            column = lax.broadcasted_iota(jnp.int32, (GROUP, MAXC), 1)
            s = jnp.where(column < lengths[r], scores[u], FLOOR)
            highest = jnp.max(s, axis=1, keepdims=True)
            w = jnp.exp2((s - highest) * SCALE2).astype(jnp.bfloat16)
            total = jnp.sum(w.astype(jnp.float32), axis=1, keepdims=True)
            c_out[r] = dot(w, cache_v[r])
            c_top[r] = jnp.broadcast_to(highest * SCALE2, (GROUP, HEAD_DIM))
            c_sum[r] = jnp.broadcast_to(total, (GROUP, HEAD_DIM))
        return 0

    lax.fori_loop(0, REQS // CACHE_GROUP, cache_step, 0)

    def attend(p, j, tasks, shift=None):
        keys = twice(kv[first + p, j, 0])
        values = with_ones(kv[first + p, j, 1])
        scores = [dot_t(keys, q_split[g, u]) for g, u in tasks]
        if shift is not None:
            key_at = lax.broadcasted_iota(jnp.int32, (BLOCK, BLOCK), 0)
            query_at = lax.broadcasted_iota(jnp.int32, (BLOCK, BLOCK), 1)
            allowed = key_at - query_at <= shift
        for (g, u), s in zip(tasks, scores):
            if shift is not None:
                s = jnp.where(allowed, s, FLOOR)
            before = top[g, u : u + 1, :]
            highest = jnp.maximum(before, jnp.max(s, axis=0, keepdims=True))
            w = jnp.exp2(s - highest).astype(jnp.bfloat16)
            acc[g, u] = acc[g, u] * jnp.exp2(before - highest) + dot(values, w)
            top[g, u : u + 1, :] = highest

    alone = jnp.where(heavy, 2, 4)
    for u in range(HALF):
        acc[alone, u] = jnp.zeros((AUG, BLOCK), jnp.float32)
    top[alone] = jnp.full((HALF, BLOCK), FLOOR, jnp.float32)

    order = (left, right, across, opposite, far_left, far_right, far_opposite)

    def block_at(k):
        j = order[0]
        for m in range(1, len(order)):
            j = jnp.where(k == m, order[m], j)
        return j

    def main_step(n, _):
        k = jnp.where(n < 4, lax.rem(n, 2), n // 2)
        p = jnp.where(n < 4, n // 2, lax.rem(n, 2))

        @pl.when(n == 2)
        def _():
            second_arrivals()

        @pl.when(n == 5)
        def _():
            opposite_arrives()

        @pl.when(jnp.logical_and(heavy, n == 8))
        def _():
            far_sides_arrive()

        @pl.when(jnp.logical_and(heavy, n == 12))
        def _():
            far_opposite_arrives()

        j = block_at(k)
        whole = jnp.logical_or(p == 0, jnp.logical_not(heavy))

        @pl.when(jnp.logical_and(j < me, whole))
        def _():
            attend(p, j, [(2 * p + h // HALF, h % HALF) for h in range(GROUP)])

        @pl.when(jnp.logical_and(j < me, jnp.logical_not(whole)))
        def _():
            attend(1, j, [(2, u) for u in range(HALF)])

        return 0

    lax.fori_loop(0, 2 * len(order), main_step, 0)

    @pl.when(jnp.logical_not(heavy))
    def _():
        lend.wait_recv()

        def split_far(u, _):
            cols = pl.ds(pl.multiple_of(u * HEAD_DIM, HEAD_DIM), HEAD_DIM)
            q_split[4, u] = split_scaled(q_far[:, cols])
            return 0

        lax.fori_loop(0, HALF, split_far, 0)

    def alone_step(n, _):
        @pl.when(n == 5)
        def _():
            far_sides_arrive()

        @pl.when(n == 7)
        def _():
            far_opposite_arrives()

        j = jnp.where(n == 0, me, block_at(n - 1))
        query_block = jnp.where(heavy, me, me + PARTNER)

        @pl.when(j <= query_block)
        def _():
            attend(1, j, [(alone, u) for u in range(HALF)], (query_block - j) * BLOCK)

        return 0

    lax.fori_loop(0, jnp.where(heavy, 1, 1 + len(order)), alone_step, 0)

    def result(g, u):
        a = acc[g, u]
        return (a[:HEAD_DIM] / a[HEAD_DIM : HEAD_DIM + 1]).T.astype(jnp.bfloat16)

    @pl.when(jnp.logical_not(heavy))
    def _():
        def finish_far(u, _):
            cols = pl.ds(pl.multiple_of(u * HEAD_DIM, HEAD_DIM), HEAD_DIM)
            out_far[:, cols] = result(4, u)
            return 0

        lax.fori_loop(0, HALF, finish_far, 0)
        give_back.start()

    def finish_step(n, _):
        g, u = n // HALF, lax.rem(n, HALF)
        cols = pl.ds(pl.multiple_of(lax.rem(n, GROUP) * HEAD_DIM, HEAD_DIM), HEAD_DIM)
        out_v[g // 2, :, cols] = result(g, u)
        return 0

    lax.fori_loop(0, jnp.where(heavy, 3 * HALF, 4 * HALF), finish_step, 0)
    near_cols = pl.ds(0, HALF * HEAD_DIM)
    out_copies = (
        pltpu.make_async_copy(out_v.at[0], out.at[0], out_sem.at[0]),
        pltpu.make_async_copy(out_v.at[1, :, near_cols], out.at[1, :, near_cols], out_sem.at[1]),
    )
    out_rest = pltpu.make_async_copy(out_v.at[1, :, far_cols], out.at[1, :, far_cols], out_sem.at[2])
    for copy in out_copies:
        copy.start()

    @pl.when(jnp.logical_not(heavy))
    def _():
        out_rest.start()

    for p in (0, 1):
        for j in range(CTX):
            shared(p, j).wait_recv()
    step_q = jnp.concatenate(
        [split_scaled(sq_in[:, h * HEAD_DIM : (h + 1) * HEAD_DIM]) for h in range(GROUP)], axis=0
    )
    width = GROUP * REQS
    request = lax.rem(lax.broadcasted_iota(jnp.int32, (1, width), 1), REQS)
    slot = jnp.zeros((1, width), jnp.int32)
    for r in range(REQS):
        slot = jnp.where(request == r, request_slot[r], slot)
    second = slot == 1
    in_second = second.astype(jnp.bfloat16)
    in_first = (1.0 - second.astype(jnp.float32)).astype(jnp.bfloat16)
    prompts = (owner_slots[0, owner], owner_slots[1, owner])
    p_acc[...] = jnp.zeros_like(p_acc)
    p_top[...] = jnp.full(p_top.shape, FLOOR, jnp.float32)

    def persona_step(i, _):
        scores = []
        for u in range(2):
            j = i * 2 + u
            a = dot_t(twice(kv[prompts[0], j, 0]), step_q)
            b = dot_t(twice(kv[prompts[1], j, 0]), step_q)
            scores.append(jnp.where(second, b, a))
        before = p_top[0:1, :]
        highest = before
        for s in scores:
            highest = jnp.maximum(highest, jnp.max(s, axis=0, keepdims=True))
        total = p_acc[...] * jnp.exp2(before - highest)
        for u in range(2):
            j = i * 2 + u
            w = jnp.exp2(scores[u] - highest).astype(jnp.bfloat16)
            total = total + dot(with_ones(kv[prompts[0], j, 1]), w * in_first)
            total = total + dot(with_ones(kv[prompts[1], j, 1]), w * in_second)
        p_acc[...] = total
        p_top[0:1, :] = highest
        return 0

    lax.fori_loop(0, CTX // 2, persona_step, 0)

    def rows(ref):
        return jnp.concatenate([ref[:, h, :] for h in range(GROUP)], axis=0)

    def spread(row):
        return jnp.broadcast_to(row, (HEAD_DIM, width)).T

    total_p, top_p = spread(p_acc[HEAD_DIM : HEAD_DIM + 1, :]), spread(p_top[0:1, :])
    top_c = rows(c_top)
    highest = jnp.maximum(top_p, top_c)
    weight_p, weight_c = jnp.exp2(top_p - highest), jnp.exp2(top_c - highest)
    mixed = p_acc[:HEAD_DIM, :].T * weight_p + rows(c_out) * weight_c
    mixed = mixed / (total_p * weight_p + rows(c_sum) * weight_c)
    for h in range(GROUP):
        step_v[:, h * HEAD_DIM : (h + 1) * HEAD_DIM] = mixed[h * REQS : (h + 1) * REQS].astype(
            jnp.bfloat16
        )
    step_copy = pltpu.make_async_copy(step_v, step_out, out_sem.at[3])
    step_copy.start()

    for sent in range(N_SENDS):
        move(sent, 0, me, left).wait_send()
    for copy in out_copies:
        copy.wait()
    step_copy.wait()

    @pl.when(heavy)
    def _():
        lend.wait_send()
        give_back.wait_recv()

    @pl.when(jnp.logical_not(heavy))
    def _():
        out_rest.wait()
        give_back.wait_send()


def on_device(pq, pk, pv, sq, ck, cv, lengths, owner_slots, request_slot):
    anywhere = pl.BlockSpec(memory_space=pl.ANY)
    scalars = pl.BlockSpec(memory_space=pltpu.SMEM)
    f32, bf16 = jnp.float32, jnp.bfloat16
    return pl.pallas_call(
        kernel,
        out_shape=(
            jax.ShapeDtypeStruct(pq.shape, bf16),
            jax.ShapeDtypeStruct(sq.shape, bf16),
        ),
        in_specs=[anywhere] * 6 + [scalars] * 3,
        out_specs=(anywhere, anywhere),
        scratch_shapes=[
            pltpu.VMEM((4, CTX, 2, BLOCK, HEAD_DIM), bf16),
            pltpu.VMEM(pq.shape, bf16),
            pltpu.VMEM((BLOCK, HALF * HEAD_DIM), bf16),
            pltpu.VMEM((5, HALF, BLOCK, 2 * HEAD_DIM), bf16),
            pltpu.VMEM((5, HALF, AUG, BLOCK), f32),
            pltpu.VMEM((5, HALF, BLOCK), f32),
            pltpu.VMEM(pq.shape, bf16),
            pltpu.VMEM((BLOCK, HALF * HEAD_DIM), bf16),
            pltpu.VMEM(ck.shape, bf16),
            pltpu.VMEM(cv.shape, bf16),
            pltpu.VMEM(sq.shape, bf16),
            pltpu.VMEM((REQS, GROUP, HEAD_DIM), f32),
            pltpu.VMEM((REQS, GROUP, HEAD_DIM), f32),
            pltpu.VMEM((REQS, GROUP, HEAD_DIM), f32),
            pltpu.VMEM((REQS, GROUP, HEAD_DIM), f32),
            pltpu.VMEM((AUG, GROUP * REQS), f32),
            pltpu.VMEM((8, GROUP * REQS), f32),
            pltpu.VMEM(sq.shape, bf16),
            pltpu.SemaphoreType.DMA((N_SENDS,)),
            pltpu.SemaphoreType.DMA((2, CTX)),
            pltpu.SemaphoreType.DMA((2, CTX)),
            pltpu.SemaphoreType.DMA((4,)),
            pltpu.SemaphoreType.DMA((6,)),
            pltpu.SemaphoreType.DMA((2, REQS // CACHE_GROUP)),
            pltpu.SemaphoreType.DMA((4,)),
        ],
        compiler_params=pltpu.CompilerParams(
            collective_id=0, has_side_effects=True, vmem_limit_bytes=60 << 20
        ),
        cost_estimate=pl.CostEstimate(
            flops=18_000_000_000, bytes_accessed=24 << 20, transcendentals=34_000_000
        ),
        name="prompt_and_step",
    )(pq, pk, pv, sq, ck, cv, lengths, owner_slots.T, request_slot)


def solution(mesh):
    in_specs = (
        P("section", "ctx", "head"),
        P("section", "ctx", "head"),
        P("section", "ctx", "head"),
        P(("section", "ctx"), "head"),
        P(("section", "ctx"), None, "head"),
        P(("section", "ctx"), None, "head"),
        P(("section", "ctx")),
        P(),
        P(("section", "ctx")),
    )
    out_specs = (P("section", "ctx", "head"), P(("section", "ctx"), "head"))
    return jax.shard_map(
        on_device, mesh=mesh, in_specs=in_specs, out_specs=out_specs, check_vma=False
    )
```

time: 75 us -> 65.5 us (0.87)
  Pallas kernels: 69.1 us -> 61 us
  local copies, waits for them, and re-layouts: 5.1 us -> 3.75 us
    pallas_call x1, Pallas kernels: 69.1 us -> 61 us  [on_device(): pl.pallas_call(kernel, out_shape=(jax.ShapeDtypeStruct(pq.shape, bf16), j...]
    unnamed x5 -> x4, local copies, waits for them, and re-layouts: 5.1 us -> 3.75 us
where the time goes in v2:
time: 65.5 us; the launch traced here: 65.4 us
  Pallas kernels  61 us (93%)
  local copies, waits for them, and re-layouts  3.75 us (6%)
    pallas_call x1, Pallas kernels, on_device(): pl.pallas_call(kernel, out_shape=(jax.ShapeDtypeStruct(pq.shape, bf16), j...  61 us
    unnamed x4, local copies, waits for them, and re-layouts  3.75 us

profile of v2, /device:TPU:30, one launch (start us, length us, event | category | flops | bytes accessed | tf_op | source)
XLA Modules:
  0.0 65.4 jit_solution(2520713862785377467)
XLA Ops:
  0.6 61.0 %prompt_and_step.1 = (bf16[2,512,1024]{2,1,0:T(8,128)(2,1)}, bf16[32,1024]{1,0:T(8,128)(2,1)}) custom-call(bf16[2,512,1024]{2,1,0:T(8,128)(2,1)} %pq.1, bf16[2,512,128]{2,1,0:T(8,128)(2,1)} %pk.1, bf16[2,512,128]{2,1,0:T(8,128)(2,1)} %pv.1, bf16[32,1024]{1,0:T(8,128)(2,1)} %sq.1, bf16[32,1024,128]{2,1,0:T(8,128)(2,1)} %ck.1, bf16[32,1024,128]{2,1,0:T(8,128)(2,1)} %cv.1, ...), custom_call_target="tpu_custom_call" | custom-call | flops 17999998976 | bytes 25165824 | tf_op jit(solution)/shard_map/prompt_and_step/pallas_call | solution.py:456
  61.6 0.0 copy-start
  61.6 3.1 %copy.13 = bf16[2,512,1024]{2,1,0:T(8,128)(2,1)} copy(bf16[2,512,1024]{2,1,0:T(8,128)(2,1)} %get-tuple-element.4) | data formatting | bytes 4194304
  64.7 0.0 copy-done
  64.7 0.6 copy.14
Async XLA Ops:
  61.6 3.1 %copy-start = (bf16[32,1024]{1,0:T(8,128)(2,1)S(1)}, bf16[32,1024]{1,0:T(8,128)(2,1)}, u32[]{:S(2)}) copy-start(bf16[32,1024]{1,0:T(8,128)(2,1)} %get-tuple-element.5) | copy-start | bytes 196612

commit v3 on v2

v3 whole, which is shorter than its diff:
```python
import jax
import jax.numpy as jnp
from jax import lax
from jax.experimental import pallas as pl
from jax.experimental.pallas import tpu as pltpu
from jax.sharding import PartitionSpec as P

HEADS = 64
KV_HEADS = 8
HEAD_DIM = 128
GROUP = HEADS // KV_HEADS
FLOOR = -1e30
SCALE2 = 1.4426950408889634 / HEAD_DIM**0.5
MESH = pl.DeviceIdType.MESH
CTX = 8
XS = 4
BLOCK = 512
REQS = 32
MAXC = 1024
CACHE_GROUP = 8
LIMIT = 2.0**100
AUG = HEAD_DIM + 16

HALF = GROUP // 2


N_SENDS = 6 + 2 + 4 + 2 + 16


def dot_t(a, b):
    return lax.dot_general(a, b, (((1,), (1,)), ((), ())), preferred_element_type=jnp.float32)


def dot(a, b):
    return lax.dot_general(a, b, (((1,), (0,)), ((), ())), preferred_element_type=jnp.float32)


def split_scaled(q):
    scaled = q.astype(jnp.float32) * SCALE2
    high = scaled.astype(jnp.bfloat16)
    low = (scaled - high.astype(jnp.float32)).astype(jnp.bfloat16)
    return jnp.concatenate([high, low], axis=1)


def twice(k):
    return jnp.concatenate([k, k], axis=1)


def with_ones(v):
    return jnp.concatenate([v.T, jnp.ones((AUG - HEAD_DIM, v.shape[0]), v.dtype)], axis=0)


def kernel(
    pq, pk, pv, sq, ck, cv, lengths, owner_slots, request_slot,
    out, step_out, kv_out, flag_out,
    kv, q_in, q_split, acc, top, out_v, bad, flag,
    cache_k, cache_v, sq_in, sq_rows,
    c_out, c_top, c_sum, sq_far, p_q, p_slot, p_acc, p_top, step_v,
    send_sem, recv_sem, sib_sem, far_sem, in_sem, cache_sem, out_sem,
):
    section = lax.axis_index("section")
    me = lax.axis_index("ctx")
    y, x = me // XS, lax.rem(me, XS)
    first = section * 2
    lends = me >= CTX - 2
    borrows = jnp.logical_and(y == 0, x >= XS - 2)

    def at(row, col):
        return row * XS + lax.rem(col + XS, XS)

    left, right = at(y, x - 1), at(y, x + 1)
    across, opposite = at(1 - y, x), at(y, x + 2)
    far_left, far_right, far_opposite = at(1 - y, x - 1), at(1 - y, x + 1), at(1 - y, x + 2)

    loads = []
    for p in (0, 1):
        for part, src in ((0, pk), (1, pv)):
            loads.append(
                pltpu.make_async_copy(src.at[p], kv.at[first + p, me, part], in_sem.at[len(loads)])
            )
    loads.append(pltpu.make_async_copy(pq, q_in, in_sem.at[4]))
    loads.append(pltpu.make_async_copy(sq, sq_in, in_sem.at[5]))
    for load in loads:
        load.start()

    def cache_copies(g):
        rows = pl.ds(g * CACHE_GROUP, CACHE_GROUP)
        return (
            pltpu.make_async_copy(ck.at[rows], cache_k.at[rows], cache_sem.at[0, g]),
            pltpu.make_async_copy(cv.at[rows], cache_v.at[rows], cache_sem.at[1, g]),
        )

    for g in range(REQS // CACHE_GROUP):
        for copy in cache_copies(g):
            copy.start()

    barrier = pltpu.get_barrier_semaphore()
    for peer in (left, right, across):
        pl.semaphore_signal(barrier, inc=1, device_id={"ctx": peer}, device_id_type=MESH)
    pl.semaphore_signal(barrier, inc=1, device_id={"section": 1 - section}, device_id_type=MESH)
    pl.semaphore_wait(barrier, 4)

    def move(slot, p, j, to):
        return pltpu.make_async_remote_copy(
            src_ref=kv.at[first + p, j],
            dst_ref=kv.at[first + p, j],
            send_sem=send_sem.at[slot],
            recv_sem=recv_sem.at[p, j],
            device_id={"ctx": to},
            device_id_type=MESH,
        )

    def share(n, p, j):
        return pltpu.make_async_remote_copy(
            src_ref=kv.at[first + p, j],
            dst_ref=kv.at[first + p, j],
            send_sem=send_sem.at[14 + 2 * n + p],
            recv_sem=sib_sem.at[p, j],
            device_id={"section": 1 - section},
            device_id_type=MESH,
        )

    def shared(p, j):
        other = kv.at[2 - first + p, j]
        return pltpu.make_async_remote_copy(
            src_ref=other, dst_ref=other, send_sem=send_sem.at[0], recv_sem=sib_sem.at[p, j],
            device_id={"section": 1 - section}, device_id_type=MESH,
        )

    def far_copy(n, src, dst):
        return pltpu.make_async_remote_copy(
            src_ref=src, dst_ref=dst, send_sem=far_sem.at[n], recv_sem=far_sem.at[4 + n],
            device_id={"ctx": across}, device_id_type=MESH,
        )

    ask = (far_copy(0, sq, sq_far), far_copy(1, p_slot.at[1], p_slot.at[0]))
    answer = (far_copy(2, p_acc.at[0], p_acc.at[1]), far_copy(3, p_top.at[0], p_top.at[1]))

    for p in (0, 1):
        loads[2 * p].wait()
        loads[2 * p + 1].wait()

        move(2 * p + 1, p, me, right).start()
        if p == 0:
            move(2 * p, p, me, left).start()
        move(4 + p, p, me, across).start()

    for p in (0, 1):
        share(0, p, me).start()

    width = GROUP * REQS
    request = lax.rem(lax.broadcasted_iota(jnp.int32, (8, width), 1), REQS)
    slot = jnp.zeros((8, width), jnp.int32)
    for r in range(REQS):
        slot = jnp.where(request == r, request_slot[r], slot)
    p_slot[1] = slot.astype(jnp.float32)

    @pl.when(lends)
    def _():
        for copy in ask:
            copy.start()

    def arrive(p, j):
        move(0, p, j, me).wait_recv()

    def arrives(n, p, j):
        arrive(p, j)
        share(n, p, j).start()

    def first_arrivals():
        arrives(3, 0, across)
        move(8, 0, across, left).start()
        move(2, 1, me, left).start()
        arrives(1, 0, left)
        move(6, 0, left, right).start()
        move(12, 0, left, across).start()
        arrives(2, 0, right)

    def second_arrivals():
        arrives(3, 1, across)
        move(9, 1, across, left).start()
        arrives(1, 1, left)
        move(13, 1, left, across).start()

    def split_step(n, _):
        g, u = n // HALF, lax.rem(n, HALF)
        h = lax.rem(n, GROUP)
        cols = pl.ds(pl.multiple_of(h * HEAD_DIM, HEAD_DIM), HEAD_DIM)
        q_split[g, u] = split_scaled(q_in[g // 2, :, cols])
        return 0

    loads[4].wait()
    lax.fori_loop(0, 4 * HALF, split_step, 0)

    def diagonal_step(p, _):
        keys = twice(kv[first + p, me, 0])
        values = with_ones(kv[first + p, me, 1])
        key_at = lax.broadcasted_iota(jnp.int32, (BLOCK, BLOCK), 0)
        query_at = lax.broadcasted_iota(jnp.int32, (BLOCK, BLOCK), 1)
        scores = [dot_t(keys, q_split[2 * p + h // HALF, h % HALF]) for h in range(GROUP)]
        for h in range(GROUP):
            g, u = 2 * p + h // HALF, h % HALF
            s = jnp.where(key_at <= query_at, scores[h], FLOOR)
            highest = jnp.max(s, axis=0, keepdims=True)
            w = jnp.exp2(s - highest).astype(jnp.bfloat16)
            acc[g, u] = dot(values, w)
            top[g, u : u + 1, :] = highest
        return 0

    lax.fori_loop(0, 2, diagonal_step, 0)


    loads[5].wait()
    for h in range(GROUP):
        sq_rows[:, h, :] = sq_in[:, h * HEAD_DIM : (h + 1) * HEAD_DIM].astype(jnp.float32)

    def cache_step(g, _):
        @pl.when(g == 2)
        def _():
            first_arrivals()

        for copy in cache_copies(g):
            copy.wait()
        scores = []
        for u in range(CACHE_GROUP):
            r = g * CACHE_GROUP + u
            scores.append(dot_t(sq_rows[r].astype(jnp.bfloat16), cache_k[r]))
        for u in range(CACHE_GROUP):
            r = g * CACHE_GROUP + u
            column = lax.broadcasted_iota(jnp.int32, (GROUP, MAXC), 1)
            s = jnp.where(column < lengths[r], scores[u], FLOOR)
            highest = jnp.max(s, axis=1, keepdims=True)
            w = jnp.exp2((s - highest) * SCALE2).astype(jnp.bfloat16)
            total = jnp.sum(w.astype(jnp.float32), axis=1, keepdims=True)
            c_out[r] = dot(w, cache_v[r])
            c_top[r] = jnp.broadcast_to(highest * SCALE2, (GROUP, HEAD_DIM))
            c_sum[r] = jnp.broadcast_to(total, (GROUP, HEAD_DIM))
        return 0

    lax.fori_loop(0, REQS // CACHE_GROUP, cache_step, 0)

    def attend(p, j, tasks):
        keys = twice(kv[first + p, j, 0])
        values = with_ones(kv[first + p, j, 1])
        scores = [dot_t(keys, q_split[g, u]) for g, u in tasks]
        for (g, u), s in zip(tasks, scores):
            w = jnp.exp2(s - top[g, u : u + 1, :]).astype(jnp.bfloat16)
            acc[g, u] += dot(values, w)

    def step_queries(ref):
        return jnp.concatenate(
            [split_scaled(ref[:, h * HEAD_DIM : (h + 1) * HEAD_DIM]) for h in range(GROUP)], axis=0
        )

    p_q[1] = step_queries(sq_in)

    @pl.when(borrows)
    def _():
        for copy in ask:
            copy.wait_recv()
        p_q[0] = step_queries(sq_far)

    def persona_step(n, _):
        t, i = n // (CTX // 2), lax.rem(n, CTX // 2)

        @pl.when(i == 0)
        def _():
            p_acc[t] = jnp.zeros((AUG, width), jnp.float32)
            p_top[t] = jnp.full((8, width), FLOOR, jnp.float32)

        owner = section * CTX + jnp.where(t == 0, across, me)
        prompts = (owner_slots[0, owner], owner_slots[1, owner])
        queries = p_q[t]
        second = p_slot[t, 0:1, :]
        in_second = second.astype(jnp.bfloat16)
        in_first = (1.0 - second).astype(jnp.bfloat16)
        scores = []
        for u in range(2):
            a = dot_t(twice(kv[prompts[0], i * 2 + u, 0]), queries)
            b = dot_t(twice(kv[prompts[1], i * 2 + u, 0]), queries)
            scores.append(jnp.where(second > 0.5, b, a))
        before = p_top[t, 0:1, :]
        highest = before
        for s in scores:
            highest = jnp.maximum(highest, jnp.max(s, axis=0, keepdims=True))
        total = p_acc[t] * jnp.exp2(before - highest)
        for u in range(2):
            w = jnp.exp2(scores[u] - highest).astype(jnp.bfloat16)
            total = total + dot(with_ones(kv[prompts[0], i * 2 + u, 1]), w * in_first)
            total = total + dot(with_ones(kv[prompts[1], i * 2 + u, 1]), w * in_second)
        p_acc[t] = total
        p_top[t, 0:1, :] = highest

        @pl.when(n == CTX // 2 - 1)
        def _():
            for copy in answer:
                copy.start()

        return 0

    bad[...] = jnp.zeros_like(bad)

    def finish(g, u, summed, total):
        cols = pl.ds(pl.multiple_of((lax.rem(g, 2) * HALF + u) * HEAD_DIM, HEAD_DIM), HEAD_DIM)
        out_v[g // 2, :, cols] = (summed * (1.0 / total)).T.astype(jnp.bfloat16)
        bad[...] = jnp.maximum(bad[...], jnp.where(total <= LIMIT, 0.0, 1.0))

    def finish_step(n, _):
        g, u = n // HALF, lax.rem(n, HALF)
        a = acc[g, u]
        finish(g, u, a[:HEAD_DIM], a[HEAD_DIM : HEAD_DIM + 1])
        return 0

    out_copies = [pltpu.make_async_copy(out_v.at[p], out.at[p], out_sem.at[p]) for p in (0, 1)]

    def pick(n, choices):
        j = choices[0]
        for m in range(1, len(choices)):
            j = jnp.where(n == m, choices[m], j)
        return j

    steps = (
        (across, 0), (left, 0), (right, 0), (across, 1), (far_right, 0), (left, 1),
        (far_left, 0), (right, 1), (opposite, 0), (far_left, 1), (far_right, 1),
        (far_opposite, 0), (far_opposite, 1), (opposite, 1),
    )

    def main_step(n, _):
        @pl.when(n == 2)
        def _():
            second_arrivals()

        @pl.when(n == 4)
        def _():
            arrives(6, 0, far_right)

        @pl.when(n == 5)
        def _():
            arrives(5, 0, far_left)
            move(10, 0, far_left, right).start()
            arrives(2, 1, right)
            move(7, 1, right, left).start()

        @pl.when(n == 8)
        def _():
            arrives(4, 0, opposite)

        @pl.when(n == 9)
        def _():
            arrives(5, 1, far_left)
            move(11, 1, far_left, right).start()

        @pl.when(n == 10)
        def _():
            arrives(6, 1, far_right)

        @pl.when(n == 11)
        def _():
            arrives(7, 0, far_opposite)

        @pl.when(n == 12)
        def _():
            lax.fori_loop(0, 2 * HALF, finish_step, 0)
            out_copies[0].start()
            arrives(7, 1, far_opposite)

        @pl.when(n == 13)
        def _():
            arrives(4, 1, opposite)

        j = pick(n, [j for j, _ in steps])
        p = pick(n, [p for _, p in steps])

        @pl.when(j < me)
        def _():
            attend(p, j, [(2 * p + h // HALF, h % HALF) for h in range(GROUP)])

        return 0

    lax.fori_loop(0, len(steps), main_step, 0)
    kv_copy = pltpu.make_async_copy(kv.at[pl.ds(first, 2)], kv_out, out_sem.at[2])
    kv_copy.start()
    lax.fori_loop(2 * HALF, 4 * HALF, finish_step, 0)
    out_copies[1].start()
    highest_bad = jnp.max(jnp.max(bad[...], axis=0, keepdims=True), axis=1, keepdims=True)
    flag[...] = jnp.broadcast_to(highest_bad, flag.shape)
    flag_copy = pltpu.make_async_copy(flag, flag_out, out_sem.at[4])
    flag_copy.start()

    for p in (0, 1):
        for j in range(CTX):
            shared(p, j).wait_recv()
    lax.fori_loop(
        jnp.where(borrows, 0, CTX // 2), jnp.where(lends, CTX // 2, CTX), persona_step, 0
    )

    @pl.when(lends)
    def _():
        for copy in answer:
            copy.wait_recv()

    def rows(ref):
        return jnp.concatenate([ref[:, h, :] for h in range(GROUP)], axis=0)

    def spread(row):
        return jnp.broadcast_to(row, (HEAD_DIM, width)).T

    top_p, top_c = spread(p_top[1, 0:1, :]), rows(c_top)
    highest = jnp.maximum(top_p, top_c)
    weight_p, weight_c = jnp.exp2(top_p - highest), jnp.exp2(top_c - highest)
    total_p = spread(p_acc[1, HEAD_DIM : HEAD_DIM + 1, :])
    mixed = p_acc[1, :HEAD_DIM, :].T * weight_p + rows(c_out) * weight_c
    mixed = mixed / (total_p * weight_p + rows(c_sum) * weight_c)
    for h in range(GROUP):
        step_v[:, h * HEAD_DIM : (h + 1) * HEAD_DIM] = mixed[h * REQS : (h + 1) * REQS].astype(
            jnp.bfloat16
        )
    step_copy = pltpu.make_async_copy(step_v, step_out, out_sem.at[3])
    step_copy.start()

    for sent in range(N_SENDS):
        move(sent, 0, me, left).wait_send()

    @pl.when(lends)
    def _():
        for copy in ask:
            copy.wait_send()

    @pl.when(borrows)
    def _():
        for copy in answer:
            copy.wait_send()

    step_copy.wait()

    for copy in out_copies:
        copy.wait()
    kv_copy.wait()
    flag_copy.wait()


def write_kernel(
    flag, out, step_out, pq, kv, result, step_result,
    held, held_step, q, rows, acc, top, in_sem, out_sem, redo_sem,
):
    pieces = 4
    length = BLOCK // pieces
    pairs = [(step_out, held_step, step_result)]
    for p in (0, 1):
        for n in range(pieces):
            pairs.append([ref.at[p, pl.ds(n * length, length)] for ref in (out, held, result)])
    reads = [pltpu.make_async_copy(a, b, in_sem.at[n]) for n, (a, b, _) in enumerate(pairs)]
    writes = [pltpu.make_async_copy(b, c, out_sem.at[n]) for n, (_, b, c) in enumerate(pairs)]
    for read in reads:
        read.start()
    for read, write in zip(reads, writes):
        read.wait()
        write.start()
    for write in writes:
        write.wait()

    @pl.when(flag[0, 0] > 0.0)
    def _():
        me = lax.axis_index("ctx")
        loads = (
            pltpu.make_async_copy(pq, q, redo_sem.at[0]),
            pltpu.make_async_copy(kv, rows, redo_sem.at[1]),
        )
        for load in loads:
            load.start()
        for load in loads:
            load.wait()

        def head_step(n, _):
            p, h = n // GROUP, lax.rem(n, GROUP)
            cols = pl.ds(pl.multiple_of(h * HEAD_DIM, HEAD_DIM), HEAD_DIM)
            queries = split_scaled(q[p, :, cols])
            acc[...] = jnp.zeros_like(acc)
            top[...] = jnp.full(top.shape, FLOOR, jnp.float32)

            def block_step(i, _):
                j = me - i
                s = dot_t(twice(rows[p, j, 0]), queries)
                key_at = lax.broadcasted_iota(jnp.int32, (BLOCK, BLOCK), 0)
                query_at = lax.broadcasted_iota(jnp.int32, (BLOCK, BLOCK), 1)
                s = jnp.where(key_at - query_at <= i * BLOCK, s, FLOOR)
                before = top[0:1, :]
                highest = jnp.maximum(before, jnp.max(s, axis=0, keepdims=True))
                w = jnp.exp2(s - highest).astype(jnp.bfloat16)
                acc[...] = acc[...] * jnp.exp2(before - highest) + dot(with_ones(rows[p, j, 1]), w)
                top[0:1, :] = highest
                return 0

            lax.fori_loop(0, me + 1, block_step, 0)
            mixed = acc[:HEAD_DIM] * (1.0 / acc[HEAD_DIM : HEAD_DIM + 1])
            held[p, :, cols] = mixed.T.astype(jnp.bfloat16)
            return 0

        lax.fori_loop(0, 2 * GROUP, head_step, 0)
        again = pltpu.make_async_copy(held, result, redo_sem.at[2])
        again.start()
        again.wait()


def write_results(flag, out, step_out, pq, kv):
    anywhere = pl.BlockSpec(memory_space=pl.ANY)
    f32, bf16 = jnp.float32, jnp.bfloat16
    return pl.pallas_call(
        write_kernel,
        out_shape=(
            jax.ShapeDtypeStruct(out.shape, out.dtype),
            jax.ShapeDtypeStruct(step_out.shape, step_out.dtype),
        ),
        in_specs=[pl.BlockSpec(memory_space=pltpu.SMEM)] + [anywhere] * 4,
        out_specs=(anywhere, anywhere),
        scratch_shapes=[
            pltpu.VMEM(out.shape, bf16),
            pltpu.VMEM(step_out.shape, bf16),
            pltpu.VMEM(pq.shape, bf16),
            pltpu.VMEM(kv.shape, bf16),
            pltpu.VMEM((AUG, BLOCK), f32),
            pltpu.VMEM((8, BLOCK), f32),
            pltpu.SemaphoreType.DMA((9,)),
            pltpu.SemaphoreType.DMA((9,)),
            pltpu.SemaphoreType.DMA((3,)),
        ],
        compiler_params=pltpu.CompilerParams(vmem_limit_bytes=60 << 20),
        name="write_results",
    )(flag, out, step_out, pq, kv)


def on_device(pq, pk, pv, sq, ck, cv, lengths, owner_slots, request_slot):
    anywhere = pl.BlockSpec(memory_space=pl.ANY)
    scalars = pl.BlockSpec(memory_space=pltpu.SMEM)
    f32, bf16 = jnp.float32, jnp.bfloat16
    out, step_out, kv, flag = pl.pallas_call(
        kernel,
        out_shape=(
            jax.ShapeDtypeStruct(pq.shape, bf16),
            jax.ShapeDtypeStruct(sq.shape, bf16),
            jax.ShapeDtypeStruct((2, CTX, 2, BLOCK, HEAD_DIM), bf16),
            jax.ShapeDtypeStruct((8, HEAD_DIM), f32),
        ),
        in_specs=[anywhere] * 6 + [scalars] * 3,
        out_specs=(anywhere,) * 4,
        scratch_shapes=[
            pltpu.VMEM((4, CTX, 2, BLOCK, HEAD_DIM), bf16),
            pltpu.VMEM(pq.shape, bf16),
            pltpu.VMEM((4, HALF, BLOCK, 2 * HEAD_DIM), bf16),
            pltpu.VMEM((4, HALF, AUG, BLOCK), f32),
            pltpu.VMEM((4, 8, BLOCK), f32),
            pltpu.VMEM(pq.shape, bf16),
            pltpu.VMEM((8, BLOCK), f32),
            pltpu.VMEM((8, HEAD_DIM), f32),
            pltpu.VMEM(ck.shape, bf16),
            pltpu.VMEM(cv.shape, bf16),
            pltpu.VMEM(sq.shape, bf16),
            pltpu.VMEM((REQS, GROUP, HEAD_DIM), f32),
            pltpu.VMEM((REQS, GROUP, HEAD_DIM), f32),
            pltpu.VMEM((REQS, GROUP, HEAD_DIM), f32),
            pltpu.VMEM((REQS, GROUP, HEAD_DIM), f32),
            pltpu.VMEM(sq.shape, bf16),
            pltpu.VMEM((2, GROUP * REQS, 2 * HEAD_DIM), bf16),
            pltpu.VMEM((2, 8, GROUP * REQS), f32),
            pltpu.VMEM((2, AUG, GROUP * REQS), f32),
            pltpu.VMEM((2, 8, GROUP * REQS), f32),
            pltpu.VMEM(sq.shape, bf16),
            pltpu.SemaphoreType.DMA((N_SENDS,)),
            pltpu.SemaphoreType.DMA((2, CTX)),
            pltpu.SemaphoreType.DMA((2, CTX)),
            pltpu.SemaphoreType.DMA((8,)),
            pltpu.SemaphoreType.DMA((6,)),
            pltpu.SemaphoreType.DMA((2, REQS // CACHE_GROUP)),
            pltpu.SemaphoreType.DMA((5,)),
        ],
        compiler_params=pltpu.CompilerParams(
            collective_id=0, has_side_effects=True, vmem_limit_bytes=60 << 20
        ),
        cost_estimate=pl.CostEstimate(
            flops=18_000_000_000, bytes_accessed=24 << 20, transcendentals=34_000_000
        ),
        name="prompt_and_step",
    )(pq, pk, pv, sq, ck, cv, lengths, owner_slots.T, request_slot)
    return write_results(flag, out, step_out, pq, kv)


def solution(mesh):
    in_specs = (
        P("section", "ctx", "head"),
        P("section", "ctx", "head"),
        P("section", "ctx", "head"),
        P(("section", "ctx"), "head"),
        P(("section", "ctx"), None, "head"),
        P(("section", "ctx"), None, "head"),
        P(("section", "ctx")),
        P(),
        P(("section", "ctx")),
    )
    out_specs = (P("section", "ctx", "head"), P(("section", "ctx"), "head"))
    return jax.shard_map(
        on_device, mesh=mesh, in_specs=in_specs, out_specs=out_specs, check_vma=False
    )
```

time: 65.5 us -> 154 us (2.35)
  Pallas kernels: 61 us -> 153 us
  local copies, waits for them, and re-layouts: 3.75 us -> 0 us
    pallas_call x0 -> x1, Pallas kernels: none -> 102 us  [write_results(): pl.pallas_call(write_kernel, out_shape=(jax.ShapeDtypeStruct(out.shape, o...]
    pallas_call x1, Pallas kernels: 61 us -> 50.8 us  [on_device(): pl.pallas_call(kernel, out_shape=(jax.ShapeDtypeStruct(pq.shape, bf16), j...]
    unnamed x4 -> x0, local copies, waits for them, and re-layouts: 3.75 us -> none
where the time goes in v3:
time: 154 us
  Pallas kernels  153 us (99%)
    pallas_call x1, Pallas kernels, write_results(): pl.pallas_call(write_kernel, out_shape=(jax.ShapeDtypeStruct(out.shape, o...  102 us
    pallas_call x1, Pallas kernels, on_device(): pl.pallas_call(kernel, out_shape=(jax.ShapeDtypeStruct(pq.shape, bf16), j...  50.8 us

profile of v3, /device:TPU:30, one launch (start us, length us, event | category | flops | bytes accessed | tf_op | source)
XLA Modules:
  0.0 153.7 jit_solution(7642447389603643376)
XLA Ops:
  0.6 50.8 %prompt_and_step.1 = (bf16[2,512,1024]{2,1,0:T(8,128)(2,1)}, bf16[32,1024]{1,0:T(8,128)(2,1)}, bf16[2,8,2,512,128]{4,3,2,1,0:T(8,128)(2,1)}, f32[8,128]{1,0:T(8,128)}) custom-call(bf16[2,512,1024]{2,1,0:T(8,128)(2,1)} %pq.3, bf16[2,512,128]{2,1,0:T(8,128)(2,1)} %pk.1, bf16[2,512,128]{2,1,0:T(8,128)(2,1)} %pv.1, bf16[32,1024]{1,0:T(8,128)(2,1)} %sq.1, ...), custom_call_target="tpu_custom_call" | custom-call | flops 17999998976 | bytes 25165824 | tf_op jit(solution)/shard_map/prompt_and_step/pallas_call | solution.py:536
  51.4 102.3 %write_results.1 = (bf16[2,512,1024]{2,1,0:T(8,128)(2,1)}, bf16[32,1024]{1,0:T(8,128)(2,1)}) custom-call(f32[8,128]{1,0:T(8,128)} %get-tuple-element.6.flag, bf16[2,512,1024]{2,1,0:T(8,128)(2,1)} %get-tuple-element.7.out, bf16[32,1024]{1,0:T(8,128)(2,1)} %get-tuple-element.8.step_out, bf16[2,512,1024]{2,1,0:T(8,128)(2,1)} %pq.3, ...), custom_call_target="tpu_custom_call" | custom-call | tf_op jit(solution)/shard_map/write_results/pallas_call | solution.py:508

commit v4 on v3

--- a/solution.py
+++ b/solution.py
@@ -55,15 +55,14 @@
     out, step_out, kv_out, flag_out,
     kv, q_in, q_split, acc, top, out_v, bad, flag,
     cache_k, cache_v, sq_in, sq_rows,
-    c_out, c_top, c_sum, sq_far, p_q, p_slot, p_acc, p_top, step_v,
-    send_sem, recv_sem, sib_sem, far_sem, in_sem, cache_sem, out_sem,
+    c_out, c_top, c_sum, p_q, p_acc, p_top, step_v,
+    send_sem, recv_sem, sib_sem, in_sem, cache_sem, out_sem,
 ):
     section = lax.axis_index("section")
     me = lax.axis_index("ctx")
     y, x = me // XS, lax.rem(me, XS)
     first = section * 2
-    lends = me >= CTX - 2
-    borrows = jnp.logical_and(y == 0, x >= XS - 2)
+    owner = section * CTX + me
 
     def at(row, col):
         return row * XS + lax.rem(col + XS, XS)
@@ -127,38 +126,16 @@
             device_id={"section": 1 - section}, device_id_type=MESH,
         )
 
-    def far_copy(n, src, dst):
-        return pltpu.make_async_remote_copy(
-            src_ref=src, dst_ref=dst, send_sem=far_sem.at[n], recv_sem=far_sem.at[4 + n],
-            device_id={"ctx": across}, device_id_type=MESH,
-        )
-
-    ask = (far_copy(0, sq, sq_far), far_copy(1, p_slot.at[1], p_slot.at[0]))
-    answer = (far_copy(2, p_acc.at[0], p_acc.at[1]), far_copy(3, p_top.at[0], p_top.at[1]))
-
     for p in (0, 1):
         loads[2 * p].wait()
         loads[2 * p + 1].wait()
 
-        move(2 * p + 1, p, me, right).start()
-        if p == 0:
-            move(2 * p, p, me, left).start()
+        for n, to in enumerate((right, left)):
+            move(2 * p + n, p, me, to).start()
         move(4 + p, p, me, across).start()
 
     for p in (0, 1):
         share(0, p, me).start()
-
-    width = GROUP * REQS
-    request = lax.rem(lax.broadcasted_iota(jnp.int32, (8, width), 1), REQS)
-    slot = jnp.zeros((8, width), jnp.int32)
-    for r in range(REQS):
-        slot = jnp.where(request == r, request_slot[r], slot)
-    p_slot[1] = slot.astype(jnp.float32)
-
-    @pl.when(lends)
-    def _():
-        for copy in ask:
-            copy.start()
 
     def arrive(p, j):
         move(0, p, j, me).wait_recv()
@@ -170,17 +147,18 @@
     def first_arrivals():
         arrives(3, 0, across)
         move(8, 0, across, left).start()
-        move(2, 1, me, left).start()
         arrives(1, 0, left)
         move(6, 0, left, right).start()
         move(12, 0, left, across).start()
         arrives(2, 0, right)
 
     def second_arrivals():
+        arrives(1, 1, left)
+        move(13, 1, left, across).start()
         arrives(3, 1, across)
         move(9, 1, across, left).start()
-        arrives(1, 1, left)
-        move(13, 1, left, across).start()
+        arrives(2, 1, right)
+        move(7, 1, right, left).start()
 
     def split_step(n, _):
         g, u = n // HALF, lax.rem(n, HALF)
@@ -195,15 +173,21 @@
     def diagonal_step(p, _):
         keys = twice(kv[first + p, me, 0])
         values = with_ones(kv[first + p, me, 1])
-        key_at = lax.broadcasted_iota(jnp.int32, (BLOCK, BLOCK), 0)
-        query_at = lax.broadcasted_iota(jnp.int32, (BLOCK, BLOCK), 1)
-        scores = [dot_t(keys, q_split[2 * p + h // HALF, h % HALF]) for h in range(GROUP)]
-        for h in range(GROUP):
-            g, u = 2 * p + h // HALF, h % HALF
-            s = jnp.where(key_at <= query_at, scores[h], FLOOR)
-            highest = jnp.max(s, axis=0, keepdims=True)
-            w = jnp.exp2(s - highest).astype(jnp.bfloat16)
-            acc[g, u] = dot(values, w)
+        middle = BLOCK // 2
+        key_at = lax.broadcasted_iota(jnp.int32, (middle, BLOCK), 0)
+        query_at = lax.broadcasted_iota(jnp.int32, (middle, BLOCK), 1)
+        allowed = key_at <= query_at
+        tasks = [(2 * p + h // HALF, h % HALF) for h in range(GROUP)]
+        first_scores = [dot_t(keys[:middle], q_split[g, u]) for g, u in tasks]
+        second_scores = [dot_t(keys[middle:], q_split[g, u, middle:, :]) for g, u in tasks]
+        for (g, u), a, b in zip(tasks, first_scores, second_scores):
+            a = jnp.where(allowed, a, FLOOR)
+            b = jnp.where(allowed[:, :middle], b, FLOOR)
+            highest = jnp.max(a, axis=0, keepdims=True)
+            late = jnp.maximum(highest[:, middle:], jnp.max(b, axis=0, keepdims=True))
+            highest = jnp.concatenate([highest[:, :middle], late], axis=1)
+            acc[g, u] = dot(values[:, :middle], jnp.exp2(a - highest).astype(jnp.bfloat16))
+            acc[g, u, :, middle:] += dot(values[:, middle:], jnp.exp2(b - late).astype(jnp.bfloat16))
             top[g, u : u + 1, :] = highest
         return 0
 
@@ -215,10 +199,6 @@
         sq_rows[:, h, :] = sq_in[:, h * HEAD_DIM : (h + 1) * HEAD_DIM].astype(jnp.float32)
 
     def cache_step(g, _):
-        @pl.when(g == 2)
-        def _():
-            first_arrivals()
-
         for copy in cache_copies(g):
             copy.wait()
         scores = []
@@ -238,6 +218,7 @@
         return 0
 
     lax.fori_loop(0, REQS // CACHE_GROUP, cache_step, 0)
+    first_arrivals()
 
     def attend(p, j, tasks):
         keys = twice(kv[first + p, j, 0])
@@ -247,55 +228,37 @@
             w = jnp.exp2(s - top[g, u : u + 1, :]).astype(jnp.bfloat16)
             acc[g, u] += dot(values, w)
 
-    def step_queries(ref):
-        return jnp.concatenate(
-            [split_scaled(ref[:, h * HEAD_DIM : (h + 1) * HEAD_DIM]) for h in range(GROUP)], axis=0
-        )
-
-    p_q[1] = step_queries(sq_in)
-
-    @pl.when(borrows)
-    def _():
-        for copy in ask:
-            copy.wait_recv()
-        p_q[0] = step_queries(sq_far)
-
-    def persona_step(n, _):
-        t, i = n // (CTX // 2), lax.rem(n, CTX // 2)
-
-        @pl.when(i == 0)
-        def _():
-            p_acc[t] = jnp.zeros((AUG, width), jnp.float32)
-            p_top[t] = jnp.full((8, width), FLOOR, jnp.float32)
-
-        owner = section * CTX + jnp.where(t == 0, across, me)
-        prompts = (owner_slots[0, owner], owner_slots[1, owner])
-        queries = p_q[t]
-        second = p_slot[t, 0:1, :]
-        in_second = second.astype(jnp.bfloat16)
-        in_first = (1.0 - second).astype(jnp.bfloat16)
+    width = GROUP * REQS
+    p_q[...] = jnp.concatenate(
+        [split_scaled(sq_in[:, h * HEAD_DIM : (h + 1) * HEAD_DIM]) for h in range(GROUP)], axis=0
+    )
+    p_acc[...] = jnp.zeros_like(p_acc)
+    p_top[...] = jnp.full(p_top.shape, FLOOR, jnp.float32)
+    request = lax.rem(lax.broadcasted_iota(jnp.int32, (1, width), 1), REQS)
+    slot = jnp.zeros((1, width), jnp.int32)
+    for r in range(REQS):
+        slot = jnp.where(request == r, request_slot[r], slot)
+    in_second = slot.astype(jnp.float32).astype(jnp.bfloat16)
+    in_first = (1 - slot).astype(jnp.float32).astype(jnp.bfloat16)
+    prompts = (owner_slots[0, owner], owner_slots[1, owner])
+
+    def persona_step(i, _):
         scores = []
         for u in range(2):
-            a = dot_t(twice(kv[prompts[0], i * 2 + u, 0]), queries)
-            b = dot_t(twice(kv[prompts[1], i * 2 + u, 0]), queries)
-            scores.append(jnp.where(second > 0.5, b, a))
-        before = p_top[t, 0:1, :]
+            a = dot_t(twice(kv[prompts[0], i * 2 + u, 0]), p_q[...])
+            b = dot_t(twice(kv[prompts[1], i * 2 + u, 0]), p_q[...])
+            scores.append(jnp.where(slot == 1, b, a))
+        before = p_top[0:1, :]
         highest = before
         for s in scores:
             highest = jnp.maximum(highest, jnp.max(s, axis=0, keepdims=True))
-        total = p_acc[t] * jnp.exp2(before - highest)
+        total = p_acc[...] * jnp.exp2(before - highest)
         for u in range(2):
             w = jnp.exp2(scores[u] - highest).astype(jnp.bfloat16)
             total = total + dot(with_ones(kv[prompts[0], i * 2 + u, 1]), w * in_first)
             total = total + dot(with_ones(kv[prompts[1], i * 2 + u, 1]), w * in_second)
-        p_acc[t] = total
-        p_top[t, 0:1, :] = highest
-
-        @pl.when(n == CTX // 2 - 1)
-        def _():
-            for copy in answer:
-                copy.start()
-
+        p_acc[...] = total
+        p_top[0:1, :] = highest
         return 0
 
     bad[...] = jnp.zeros_like(bad)
@@ -320,9 +283,9 @@
         return j
 
     steps = (
-        (across, 0), (left, 0), (right, 0), (across, 1), (far_right, 0), (left, 1),
-        (far_left, 0), (right, 1), (opposite, 0), (far_left, 1), (far_right, 1),
-        (far_opposite, 0), (far_opposite, 1), (opposite, 1),
+        (across, 0), (left, 0), (right, 0), (across, 1), (left, 1), (right, 1),
+        (opposite, 0), (far_right, 0), (far_left, 0), (far_left, 1), (far_right, 1),
+        (far_opposite, 0), (opposite, 1), (far_opposite, 1),
     )
 
     def main_step(n, _):
@@ -330,22 +293,17 @@
         def _():
             second_arrivals()
 
-        @pl.when(n == 4)
-        def _():
-            arrives(6, 0, far_right)
-
-        @pl.when(n == 5)
+        @pl.when(n == 6)
         def _():
             arrives(5, 0, far_left)
             move(10, 0, far_left, right).start()
-            arrives(2, 1, right)
-            move(7, 1, right, left).start()
+            arrives(4, 0, opposite)
+
+        @pl.when(n == 7)
+        def _():
+            arrives(6, 0, far_right)
 
         @pl.when(n == 8)
-        def _():
-            arrives(4, 0, opposite)
-
-        @pl.when(n == 9)
         def _():
             arrives(5, 1, far_left)
             move(11, 1, far_left, right).start()
@@ -362,11 +320,11 @@
         def _():
             lax.fori_loop(0, 2 * HALF, finish_step, 0)
             out_copies[0].start()
+            arrives(4, 1, opposite)
+
+        @pl.when(n == 13)
+        def _():
             arrives(7, 1, far_opposite)
-
-        @pl.when(n == 13)
-        def _():
-            arrives(4, 1, opposite)
 
         j = pick(n, [j for j, _ in steps])
         p = pick(n, [p for _, p in steps])
@@ -390,14 +348,7 @@
     for p in (0, 1):
         for j in range(CTX):
             shared(p, j).wait_recv()
-    lax.fori_loop(
-        jnp.where(borrows, 0, CTX // 2), jnp.where(lends, CTX // 2, CTX), persona_step, 0
-    )
-
-    @pl.when(lends)
-    def _():
-        for copy in answer:
-            copy.wait_recv()
+    lax.fori_loop(0, CTX // 2, persona_step, 0)
 
     def rows(ref):
         return jnp.concatenate([ref[:, h, :] for h in range(GROUP)], axis=0)
@@ -405,11 +356,11 @@
     def spread(row):
         return jnp.broadcast_to(row, (HEAD_DIM, width)).T
 
-    top_p, top_c = spread(p_top[1, 0:1, :]), rows(c_top)
+    top_p, top_c = spread(p_top[0:1, :]), rows(c_top)
     highest = jnp.maximum(top_p, top_c)
     weight_p, weight_c = jnp.exp2(top_p - highest), jnp.exp2(top_c - highest)
-    total_p = spread(p_acc[1, HEAD_DIM : HEAD_DIM + 1, :])
-    mixed = p_acc[1, :HEAD_DIM, :].T * weight_p + rows(c_out) * weight_c
+    total_p = spread(p_acc[HEAD_DIM : HEAD_DIM + 1, :])
+    mixed = p_acc[:HEAD_DIM, :].T * weight_p + rows(c_out) * weight_c
     mixed = mixed / (total_p * weight_p + rows(c_sum) * weight_c)
     for h in range(GROUP):
         step_v[:, h * HEAD_DIM : (h + 1) * HEAD_DIM] = mixed[h * REQS : (h + 1) * REQS].astype(
@@ -421,16 +372,6 @@
     for sent in range(N_SENDS):
         move(sent, 0, me, left).wait_send()
 
-    @pl.when(lends)
-    def _():
-        for copy in ask:
-            copy.wait_send()
-
-    @pl.when(borrows)
-    def _():
-        for copy in answer:
-            copy.wait_send()
-
     step_copy.wait()
 
     for copy in out_copies:
@@ -441,7 +382,7 @@
 
 def write_kernel(
     flag, out, step_out, pq, kv, result, step_result,
-    held, held_step, q, rows, acc, top, in_sem, out_sem, redo_sem,
+    flag_in, held, held_step, q, rows, acc, top, in_sem, out_sem, redo_sem,
 ):
     pieces = 4
     length = BLOCK // pieces
@@ -453,13 +394,17 @@
     writes = [pltpu.make_async_copy(b, c, out_sem.at[n]) for n, (_, b, c) in enumerate(pairs)]
     for read in reads:
         read.start()
+    flag_read = pltpu.make_async_copy(flag, flag_in, redo_sem.at[3])
+    flag_read.start()
     for read, write in zip(reads, writes):
         read.wait()
         write.start()
     for write in writes:
         write.wait()
 
-    @pl.when(flag[0, 0] > 0.0)
+    flag_read.wait()
+
+    @pl.when(flag_in[0, 0] > 0.0)
     def _():
         me = lax.axis_index("ctx")
         loads = (
@@ -511,9 +456,10 @@
             jax.ShapeDtypeStruct(out.shape, out.dtype),
             jax.ShapeDtypeStruct(step_out.shape, step_out.dtype),
         ),
-        in_specs=[pl.BlockSpec(memory_space=pltpu.SMEM)] + [anywhere] * 4,
+        in_specs=[anywhere] * 5,
         out_specs=(anywhere, anywhere),
         scratch_shapes=[
+            pltpu.SMEM(flag.shape, f32),
             pltpu.VMEM(out.shape, bf16),
             pltpu.VMEM(step_out.shape, bf16),
             pltpu.VMEM(pq.shape, bf16),
@@ -522,7 +468,7 @@
             pltpu.VMEM((8, BLOCK), f32),
             pltpu.SemaphoreType.DMA((9,)),
             pltpu.SemaphoreType.DMA((9,)),
-            pltpu.SemaphoreType.DMA((3,)),
+            pltpu.SemaphoreType.DMA((4,)),
         ],
         compiler_params=pltpu.CompilerParams(vmem_limit_bytes=60 << 20),
         name="write_results",
@@ -559,16 +505,13 @@
             pltpu.VMEM((REQS, GROUP, HEAD_DIM), f32),
             pltpu.VMEM((REQS, GROUP, HEAD_DIM), f32),
             pltpu.VMEM((REQS, GROUP, HEAD_DIM), f32),
-            pltpu.VMEM(sq.shape, bf16),
-            pltpu.VMEM((2, GROUP * REQS, 2 * HEAD_DIM), bf16),
-            pltpu.VMEM((2, 8, GROUP * REQS), f32),
-            pltpu.VMEM((2, AUG, GROUP * REQS), f32),
-            pltpu.VMEM((2, 8, GROUP * REQS), f32),
+            pltpu.VMEM((GROUP * REQS, 2 * HEAD_DIM), bf16),
+            pltpu.VMEM((AUG, GROUP * REQS), f32),
+            pltpu.VMEM((8, GROUP * REQS), f32),
             pltpu.VMEM(sq.shape, bf16),
             pltpu.SemaphoreType.DMA((N_SENDS,)),
             pltpu.SemaphoreType.DMA((2, CTX)),
             pltpu.SemaphoreType.DMA((2, CTX)),
-            pltpu.SemaphoreType.DMA((8,)),
             pltpu.SemaphoreType.DMA((6,)),
             pltpu.SemaphoreType.DMA((2, REQS // CACHE_GROUP)),
             pltpu.SemaphoreType.DMA((5,)),

time: 154 us -> 154 us (level)
  no operation moved by 1% of the time
where the time goes in v4:
time: 154 us
  Pallas kernels  153 us (99%)
    pallas_call x1, Pallas kernels, write_results(): pl.pallas_call(write_kernel, out_shape=(jax.ShapeDtypeStruct(out.shape, o...  102 us
    pallas_call x1, Pallas kernels, on_device(): pl.pallas_call(kernel, out_shape=(jax.ShapeDtypeStruct(pq.shape, bf16), j...  51.7 us

profile of v4, /device:TPU:30, one launch (start us, length us, event | category | flops | bytes accessed | tf_op | source)
XLA Modules:
  0.0 153.9 jit_solution(7770301153865146094)
XLA Ops:
  0.6 51.7 %prompt_and_step.1 = (bf16[2,512,1024]{2,1,0:T(8,128)(2,1)}, bf16[32,1024]{1,0:T(8,128)(2,1)}, bf16[2,8,2,512,128]{4,3,2,1,0:T(8,128)(2,1)}, f32[8,128]{1,0:T(8,128)}) custom-call(bf16[2,512,1024]{2,1,0:T(8,128)(2,1)} %pq.3, bf16[2,512,128]{2,1,0:T(8,128)(2,1)} %pk.1, bf16[2,512,128]{2,1,0:T(8,128)(2,1)} %pv.1, bf16[32,1024]{1,0:T(8,128)(2,1)} %sq.1, ...), custom_call_target="tpu_custom_call" | custom-call | flops 17999998976 | bytes 25165824 | tf_op jit(solution)/shard_map/prompt_and_step/pallas_call | solution.py:482
  52.3 101.6 %write_results.1 = (bf16[2,512,1024]{2,1,0:T(8,128)(2,1)}, bf16[32,1024]{1,0:T(8,128)(2,1)}) custom-call(f32[8,128]{1,0:T(8,128)} %get-tuple-element.6.flag, bf16[2,512,1024]{2,1,0:T(8,128)(2,1)} %get-tuple-element.7.out, bf16[32,1024]{1,0:T(8,128)(2,1)} %get-tuple-element.8.step_out, bf16[2,512,1024]{2,1,0:T(8,128)(2,1)} %pq.3, ...), custom_call_target="tpu_custom_call" | custom-call | tf_op jit(solution)/shard_map/write_results/pallas_call | solution.py:453

commit v5 on v3

--- a/solution.py
+++ b/solution.py
@@ -140,9 +140,8 @@
         loads[2 * p].wait()
         loads[2 * p + 1].wait()
 
-        move(2 * p + 1, p, me, right).start()
-        if p == 0:
-            move(2 * p, p, me, left).start()
+        for n, to in enumerate((right, left)):
+            move(2 * p + n, p, me, to).start()
         move(4 + p, p, me, across).start()
 
     for p in (0, 1):
@@ -170,17 +169,18 @@
     def first_arrivals():
         arrives(3, 0, across)
         move(8, 0, across, left).start()
-        move(2, 1, me, left).start()
         arrives(1, 0, left)
         move(6, 0, left, right).start()
         move(12, 0, left, across).start()
         arrives(2, 0, right)
 
     def second_arrivals():
+        arrives(1, 1, left)
+        move(13, 1, left, across).start()
         arrives(3, 1, across)
         move(9, 1, across, left).start()
-        arrives(1, 1, left)
-        move(13, 1, left, across).start()
+        arrives(2, 1, right)
+        move(7, 1, right, left).start()
 
     def split_step(n, _):
         g, u = n // HALF, lax.rem(n, HALF)
@@ -195,15 +195,21 @@
     def diagonal_step(p, _):
         keys = twice(kv[first + p, me, 0])
         values = with_ones(kv[first + p, me, 1])
-        key_at = lax.broadcasted_iota(jnp.int32, (BLOCK, BLOCK), 0)
-        query_at = lax.broadcasted_iota(jnp.int32, (BLOCK, BLOCK), 1)
-        scores = [dot_t(keys, q_split[2 * p + h // HALF, h % HALF]) for h in range(GROUP)]
-        for h in range(GROUP):
-            g, u = 2 * p + h // HALF, h % HALF
-            s = jnp.where(key_at <= query_at, scores[h], FLOOR)
-            highest = jnp.max(s, axis=0, keepdims=True)
-            w = jnp.exp2(s - highest).astype(jnp.bfloat16)
-            acc[g, u] = dot(values, w)
+        middle = BLOCK // 2
+        key_at = lax.broadcasted_iota(jnp.int32, (middle, BLOCK), 0)
+        query_at = lax.broadcasted_iota(jnp.int32, (middle, BLOCK), 1)
+        allowed = key_at <= query_at
+        tasks = [(2 * p + h // HALF, h % HALF) for h in range(GROUP)]
+        first_scores = [dot_t(keys[:middle], q_split[g, u]) for g, u in tasks]
+        second_scores = [dot_t(keys[middle:], q_split[g, u, middle:, :]) for g, u in tasks]
+        for (g, u), a, b in zip(tasks, first_scores, second_scores):
+            a = jnp.where(allowed, a, FLOOR)
+            b = jnp.where(allowed[:, :middle], b, FLOOR)
+            highest = jnp.max(a, axis=0, keepdims=True)
+            late = jnp.maximum(highest[:, middle:], jnp.max(b, axis=0, keepdims=True))
+            highest = jnp.concatenate([highest[:, :middle], late], axis=1)
+            acc[g, u] = dot(values[:, :middle], jnp.exp2(a - highest).astype(jnp.bfloat16))
+            acc[g, u, :, middle:] += dot(values[:, middle:], jnp.exp2(b - late).astype(jnp.bfloat16))
             top[g, u : u + 1, :] = highest
         return 0
 
@@ -215,10 +221,6 @@
         sq_rows[:, h, :] = sq_in[:, h * HEAD_DIM : (h + 1) * HEAD_DIM].astype(jnp.float32)
 
     def cache_step(g, _):
-        @pl.when(g == 2)
-        def _():
-            first_arrivals()
-
         for copy in cache_copies(g):
             copy.wait()
         scores = []
@@ -238,6 +240,7 @@
         return 0
 
     lax.fori_loop(0, REQS // CACHE_GROUP, cache_step, 0)
+    first_arrivals()
 
     def attend(p, j, tasks):
         keys = twice(kv[first + p, j, 0])
@@ -253,12 +256,6 @@
         )
 
     p_q[1] = step_queries(sq_in)
-
-    @pl.when(borrows)
-    def _():
-        for copy in ask:
-            copy.wait_recv()
-        p_q[0] = step_queries(sq_far)
 
     def persona_step(n, _):
         t, i = n // (CTX // 2), lax.rem(n, CTX // 2)
@@ -320,9 +317,9 @@
         return j
 
     steps = (
-        (across, 0), (left, 0), (right, 0), (across, 1), (far_right, 0), (left, 1),
-        (far_left, 0), (right, 1), (opposite, 0), (far_left, 1), (far_right, 1),
-        (far_opposite, 0), (far_opposite, 1), (opposite, 1),
+        (across, 0), (left, 0), (right, 0), (across, 1), (left, 1), (right, 1),
+        (opposite, 0), (far_right, 0), (far_left, 0), (far_left, 1), (far_right, 1),
+        (far_opposite, 0), (opposite, 1), (far_opposite, 1),
     )
 
     def main_step(n, _):
@@ -330,22 +327,20 @@
         def _():
             second_arrivals()
 
-        @pl.when(n == 4)
-        def _():
-            arrives(6, 0, far_right)
-
         @pl.when(n == 5)
         def _():
             arrives(5, 0, far_left)
             move(10, 0, far_left, right).start()
-            arrives(2, 1, right)
-            move(7, 1, right, left).start()
-
-        @pl.when(n == 8)
+
+        @pl.when(n == 6)
         def _():
             arrives(4, 0, opposite)
 
-        @pl.when(n == 9)
+        @pl.when(n == 7)
+        def _():
+            arrives(6, 0, far_right)
+
+        @pl.when(n == 7)
         def _():
             arrives(5, 1, far_left)
             move(11, 1, far_left, right).start()
@@ -362,11 +357,11 @@
         def _():
             lax.fori_loop(0, 2 * HALF, finish_step, 0)
             out_copies[0].start()
+            arrives(4, 1, opposite)
+
+        @pl.when(n == 13)
+        def _():
             arrives(7, 1, far_opposite)
-
-        @pl.when(n == 13)
-        def _():
-            arrives(4, 1, opposite)
 
         j = pick(n, [j for j, _ in steps])
         p = pick(n, [p for _, p in steps])
@@ -390,6 +385,12 @@
     for p in (0, 1):
         for j in range(CTX):
             shared(p, j).wait_recv()
+    @pl.when(borrows)
+    def _():
+        for copy in ask:
+            copy.wait_recv()
+        p_q[0] = step_queries(sq_far)
+
     lax.fori_loop(
         jnp.where(borrows, 0, CTX // 2), jnp.where(lends, CTX // 2, CTX), persona_step, 0
     )
@@ -441,7 +442,7 @@
 
 def write_kernel(
     flag, out, step_out, pq, kv, result, step_result,
-    held, held_step, q, rows, acc, top, in_sem, out_sem, redo_sem,
+    flag_in, held, held_step, q, rows, acc, top, in_sem, out_sem, redo_sem,
 ):
     pieces = 4
     length = BLOCK // pieces
@@ -453,13 +454,17 @@
     writes = [pltpu.make_async_copy(b, c, out_sem.at[n]) for n, (_, b, c) in enumerate(pairs)]
     for read in reads:
         read.start()
+    flag_read = pltpu.make_async_copy(flag, flag_in, redo_sem.at[3])
+    flag_read.start()
     for read, write in zip(reads, writes):
         read.wait()
         write.start()
     for write in writes:
         write.wait()
 
-    @pl.when(flag[0, 0] > 0.0)
+    flag_read.wait()
+
+    @pl.when(flag_in[0, 0] > 0.0)
     def _():
         me = lax.axis_index("ctx")
         loads = (
@@ -511,9 +516,10 @@
             jax.ShapeDtypeStruct(out.shape, out.dtype),
             jax.ShapeDtypeStruct(step_out.shape, step_out.dtype),
         ),
-        in_specs=[pl.BlockSpec(memory_space=pltpu.SMEM)] + [anywhere] * 4,
+        in_specs=[anywhere] * 5,
         out_specs=(anywhere, anywhere),
         scratch_shapes=[
+            pltpu.SMEM(flag.shape, f32),
             pltpu.VMEM(out.shape, bf16),
             pltpu.VMEM(step_out.shape, bf16),
             pltpu.VMEM(pq.shape, bf16),
@@ -522,7 +528,7 @@
             pltpu.VMEM((8, BLOCK), f32),
             pltpu.SemaphoreType.DMA((9,)),
             pltpu.SemaphoreType.DMA((9,)),
-            pltpu.SemaphoreType.DMA((3,)),
+            pltpu.SemaphoreType.DMA((4,)),
         ],
         compiler_params=pltpu.CompilerParams(vmem_limit_bytes=60 << 20),
         name="write_results",

time: 154 us -> 153 us (level)
  no operation moved by 1% of the time
where the time goes in v5:
time: 153 us
  Pallas kernels  152 us (99%)
    pallas_call x1, Pallas kernels, write_results(): pl.pallas_call(write_kernel, out_shape=(jax.ShapeDtypeStruct(out.shape, o...  102 us
    pallas_call x1, Pallas kernels, on_device(): pl.pallas_call(kernel, out_shape=(jax.ShapeDtypeStruct(pq.shape, bf16), j...  50.2 us

profile of v5, /device:TPU:30, one launch (start us, length us, event | category | flops | bytes accessed | tf_op | source)
XLA Modules:
  0.0 152.5 jit_solution(2022633433086501873)
XLA Ops:
  0.6 50.2 %prompt_and_step.1 = (bf16[2,512,1024]{2,1,0:T(8,128)(2,1)}, bf16[32,1024]{1,0:T(8,128)(2,1)}, bf16[2,8,2,512,128]{4,3,2,1,0:T(8,128)(2,1)}, f32[8,128]{1,0:T(8,128)}) custom-call(bf16[2,512,1024]{2,1,0:T(8,128)(2,1)} %pq.3, bf16[2,512,128]{2,1,0:T(8,128)(2,1)} %pk.1, bf16[2,512,128]{2,1,0:T(8,128)(2,1)} %pv.1, bf16[32,1024]{1,0:T(8,128)(2,1)} %sq.1, ...), custom_call_target="tpu_custom_call" | custom-call | flops 17999998976 | bytes 25165824 | tf_op jit(solution)/shard_map/prompt_and_step/pallas_call | solution.py:542
  50.9 101.6 %write_results.1 = (bf16[2,512,1024]{2,1,0:T(8,128)(2,1)}, bf16[32,1024]{1,0:T(8,128)(2,1)}) custom-call(f32[8,128]{1,0:T(8,128)} %get-tuple-element.6.flag, bf16[2,512,1024]{2,1,0:T(8,128)(2,1)} %get-tuple-element.7.out, bf16[32,1024]{1,0:T(8,128)(2,1)} %get-tuple-element.8.step_out, bf16[2,512,1024]{2,1,0:T(8,128)(2,1)} %pq.3, ...), custom_call_target="tpu_custom_call" | custom-call | tf_op jit(solution)/shard_map/write_results/pallas_call | solution.py:513
